TPU v7x, 256 devices: a whole 4x4x8 slice. The times are simulated.
256 devices in a mesh: dp: 8 (over x, core), context: 32 (over z, y).
Axes of the slice: x: 4, y: 4, z: 8, core: 2. Of those that a mesh axis runs over, the one named last changes fastest.
Arguments:
- tokens: bfloat16 [8, 8192, 2048], P('dp', 'context'), may hold values from -6 to 6
- weight: bfloat16 [2048, 2048], P('context'), may hold values from -0.125 to 0.125
- gate: bfloat16 [8, 8192, 2048], P('dp', 'context'), may hold values from -6 to 6
- skip: float32 [2048], replicated, may hold values from 0.1 to 1.9
- first_factor: bfloat16 [64, 128, 128], P('context'), may hold values from -0.5 to 0.5
- second_factor: bfloat16 [128, 64, 64], P('context'), may hold values from -0.75 to 0.75
- kernel: bfloat16 [64, 128, 2048], P(None, 'context'), may hold values from -6 to 6
- third_factor: bfloat16 [128, 64, 64], P('context'), may hold values from -0.75 to 0.75
- fourth_factor: bfloat16 [64, 128, 128], P('context'), may hold values from -0.5 to 0.5
- cotangent: bfloat16 [8, 8192, 2048], P('dp', 'context'), may hold values from -6 to 6
Outputs:
- mixed: bfloat16 [8, 8192, 2048], P('dp', 'context')
- grad_tokens: bfloat16 [8, 8192, 2048], P('dp', 'context')
- grad_gate: bfloat16 [8, 8192, 2048], P('dp', 'context')
- grad_weight: float32 [2048, 2048], P('context')
All inputs are finite; a program needn't handle non-finite values.
Results may differ from a plain program's by a relative error of at most 0.019.
Values may be sent and summed in bfloat16 or wider, within the bound.
A program may use at most 128 MiB of HBM per device.

v0:
```python
import jax
import jax.numpy as jnp
from jax import lax
from jax.sharding import PartitionSpec as P


def forward_columns(columns_in, second_factor, kern, third_factor):
    second_mix = jnp.einsum(
        "stq,qsc->tsc", second_factor, columns_in, preferred_element_type=jnp.float32
    )
    filtered = (second_mix * kern).astype(jnp.bfloat16)
    return jnp.einsum(
        "spt,tsc->psc", third_factor, filtered, preferred_element_type=jnp.float32
    ).astype(jnp.bfloat16)


def backward_columns(grad_cols, second_factor, kern, third_factor):
    grad_filtered_in = jnp.einsum(
        "spt,psc->tsc", third_factor, grad_cols, preferred_element_type=jnp.float32
    )
    grad_second = (grad_filtered_in * kern).astype(jnp.bfloat16)
    return jnp.einsum(
        "stq,tsc->qsc", second_factor, grad_second, preferred_element_type=jnp.float32
    ).astype(jnp.bfloat16)


def per_device(
    tokens,
    weight,
    gate,
    skip,
    first_factor,
    second_factor,
    kernel,
    third_factor,
    fourth_factor,
    cotangent,
):
    local_tokens = tokens[0]
    row_count = local_tokens.shape[0]
    feat_width = local_tokens.shape[1]
    block_size = first_factor.shape[1]
    local_blocks = row_count // block_size
    columns = local_tokens
    proj_full = jnp.dot(
        columns,
        lax.all_gather(weight, "context", axis=0, tiled=True),
        preferred_element_type=jnp.float32,
    )
    proj = proj_full.astype(jnp.bfloat16)
    proj_blocks = proj.reshape(local_blocks, block_size, feat_width)
    gate_vals = gate[0].astype(jnp.float32)
    out_grad = cotangent[0].astype(jnp.float32)
    gated_grad = (out_grad * gate_vals).astype(jnp.bfloat16)
    kern = kernel.astype(jnp.float32)
    first_mix = jnp.einsum(
        "qsr,qrc->qsc", first_factor, proj_blocks, preferred_element_type=jnp.float32
    ).astype(jnp.bfloat16)
    grad_third = jnp.einsum(
        "qrs,qrc->qsc",
        fourth_factor,
        gated_grad.reshape(local_blocks, block_size, feat_width),
        preferred_element_type=jnp.float32,
    ).astype(jnp.bfloat16)
    columns_in = lax.all_to_all(first_mix, "context", split_axis=1, concat_axis=0, tiled=True)
    third_mix = forward_columns(columns_in, second_factor, kern, third_factor)
    rows_back = lax.all_to_all(third_mix, "context", split_axis=0, concat_axis=1, tiled=True)
    grad_cols = lax.all_to_all(grad_third, "context", split_axis=1, concat_axis=0, tiled=True)
    grad_first = backward_columns(grad_cols, second_factor, kern, third_factor)
    grad_rows_in = lax.all_to_all(grad_first, "context", split_axis=0, concat_axis=1, tiled=True)
    field = jnp.einsum(
        "qrs,qsc->qrc", fourth_factor, rows_back, preferred_element_type=jnp.float32
    ).reshape(row_count, feat_width)
    pre_gate = field + skip * proj.astype(jnp.float32)
    mixed = (gate_vals * pre_gate).astype(jnp.bfloat16)
    grad_gate = (out_grad * pre_gate).astype(jnp.bfloat16)
    grad_field = jnp.einsum(
        "qsr,qsc->qrc", first_factor, grad_rows_in, preferred_element_type=jnp.float32
    ).reshape(row_count, feat_width)
    grad_proj = (grad_field + skip * gated_grad.astype(jnp.float32)).astype(jnp.bfloat16)
    grad_tokens = jnp.einsum(
        "tc,ic->ti",
        grad_proj,
        lax.all_gather(weight, "context", axis=0, tiled=True),
        preferred_element_type=jnp.float32,
    ).astype(jnp.bfloat16)
    columns = local_tokens
    partial_rows = lax.psum_scatter(
        jnp.einsum("ti,tc->ic", columns, grad_proj, preferred_element_type=jnp.float32).astype(
            jnp.bfloat16
        ),
        "context",
        scatter_dimension=0,
        tiled=True,
    )
    grad_weight = lax.psum(partial_rows, "dp").astype(jnp.float32)
    return (mixed[None], grad_tokens[None], grad_gate[None], grad_weight)


def solution(mesh):
    in_specs = (
        P("dp", "context", None),
        P("context", None),
        P("dp", "context", None),
        P(),
        P("context", None, None),
        P("context", None, None),
        P(None, "context", None),
        P("context", None, None),
        P("context", None, None),
        P("dp", "context", None),
    )
    out_specs = (
        P("dp", "context", None),
        P("dp", "context", None),
        P("dp", "context", None),
        P("context", None),
    )
    return jax.shard_map(
        per_device, mesh=mesh, in_specs=in_specs, out_specs=out_specs, check_vma=False
    )
```

profile of v0, /device:TPU:1, one launch (start us, length us, event | category | flops | bytes accessed | tf_op | source)
XLA Modules:
  0.0 463.0 jit_solution(14560172469387998406)
XLA Ops:
  7.2 0.0 copy-start
  7.2 0.0 copy-start.5
  7.2 0.0 all-gather.2.cloned.1.call-start
  7.2 0.7 all-gather.2.cloned.1.call-update
  7.9 0.0 reduce-scatter.4.cloned.1.call-start
  8.0 1.9 fusion.15
  9.9 0.0 copy-done.5
  9.9 1.5 fusion.9
  11.4 2.6 copy.44
  14.0 0.0 copy-start.7
  14.0 0.0 copy-start.8
  14.0 45.7 %all_to_all.72 = bf16[2,128,2048]{2,0,1:T(2,128)(2,1)S(1)} all-to-all(bf16[2,128,2048]{2,0,1:T(2,128)(2,1)S(1)} %copy.44), channel_id=1, replica_groups=mesh['dp'=8,'context'=32] {'context'}, dimensions={1} | all-to-all | bytes 2097152 | tf_op jit(solution)/shard_map/all_to_all | solution.py:68
  59.8 1.5 copy.45
  61.3 0.0 copy-done.7
  61.3 0.0 copy-done.8
  61.3 0.0 copy-done.4
  61.3 5.1 %fusion.10 = bf16[64,4,2048]{2,0,1:T(8,128)(2,1)} fusion(bf16[4,64,64]{2,1,0:T(8,128)(2,1)S(1)} %copy-done.8, bf16[4,64,64]{2,1,0:T(8,128)(2,1)S(1)} %copy-done.7, bf16[64,4,2048]{2,1,0:T(4,128)(2,1)} %bitcast.125, bf16[64,4,2048]{2,1,0:T(4,128)(2,1)S(1)} %copy-done.4), kind=kOutput, calls=%fused_computation.22 | convolution fusion | flops 136314880 | bytes 3211264 | tf_op jit(solution)/shard_map/stq,tsc->qsc/dot_general | solution.py:22
  66.4 2.0 copy.49
  68.4 46.2 %all_to_all.73 = bf16[64,4,2048]{2,1,0:T(4,128)(2,1)S(1)} all-to-all(bf16[64,4,2048]{2,1,0:T(4,128)(2,1)S(1)} %copy.49), channel_id=1, replica_groups=mesh['dp'=8,'context'=32] {'context'}, dimensions={0} | all-to-all | bytes 2097152 | tf_op jit(solution)/shard_map/all_to_all | solution.py:70
  114.6 0.5 copy.76
  115.1 1.1 all_to_all.67
  116.2 3.1 fusion.17
  119.3 5.6 %convert_bitcast_fusion = bf16[2048,2048]{0,1:T(8,128)(2,1)} fusion(bf16[256,2048]{1,0:T(8,128)(2,1)S(1)} %bitcast.114, bf16[1,256,2048]{2,1,0:T(8,128)(2,1)S(1)} %copy-done), kind=kOutput, calls=%fused_computation | convolution fusion | flops 2151677952 | bytes 10485760 | tf_op jit(solution)/shard_map/ti,tc->ic/dot_general | solution.py:89
  124.9 12.4 %copy.58 = bf16[2048,2048]{1,0:T(8,128)(2,1)} copy(bf16[2048,2048]{0,1:T(8,128)(2,1)} %convert_bitcast_fusion) | data formatting | bytes 16777216
  137.3 0.0 reduce-scatter.4.cloned.1.call-update
  137.4 0.2 all-reduce.2.cloned.1.call-start
  137.6 3.2 all-gather.2.cloned.1.call-done
  140.8 5.7 %convolution_convert_fusion.5 = bf16[256,2048]{1,0:T(8,128)(2,1)S(1)} fusion(bf16[2048,2048]{1,0:T(8,128)(2,1)} %all-gather.2.cloned.1.call-done, bf16[1,256,2048]{2,1,0:T(8,128)(2,1)S(1)} %copy-done), kind=kOutput, calls=%fused_computation.18 | convolution fusion | flops 2148007936 | bytes 10485760 | tf_op jit(solution)/shard_map/dot_general | solution.py:45
  146.5 1.5 fusion.8
  148.0 2.6 copy.37
  150.6 40.9 %all_to_all.74 = bf16[2,128,2048]{2,0,1:T(2,128)(2,1)S(1)} all-to-all(bf16[2,128,2048]{2,0,1:T(2,128)(2,1)S(1)} %copy.37), channel_id=1, replica_groups=mesh['dp'=8,'context'=32] {'context'}, dimensions={1} | all-to-all | bytes 2097152 | tf_op jit(solution)/shard_map/all_to_all | solution.py:65
  191.6 0.5 copy.38
  192.1 5.1 %fusion.11 = bf16[64,4,2048]{2,0,1:T(8,128)(2,1)} fusion(bf16[4,64,64]{2,1,0:T(8,128)(2,1)S(1)} %copy-done.7, bf16[4,64,64]{2,1,0:T(8,128)(2,1)S(1)} %copy-done.8, bf16[64,4,2048]{2,1,0:T(4,128)(2,1)S(1)} %bitcast.116, bf16[64,4,2048]{2,1,0:T(4,128)(2,1)} %param.16), kind=kOutput, calls=%fused_computation.23 | convolution fusion | flops 136314880 | bytes 3211264 | tf_op jit(solution)/shard_map/spt,tsc->psc/dot_general | solution.py:12
  197.2 2.0 copy.41
  199.2 40.2 %all_to_all.75 = bf16[64,4,2048]{2,1,0:T(4,128)(2,1)S(1)} all-to-all(bf16[64,4,2048]{2,1,0:T(4,128)(2,1)S(1)} %copy.41), channel_id=1, replica_groups=mesh['dp'=8,'context'=32] {'context'}, dimensions={0} | all-to-all | bytes 2097152 | tf_op jit(solution)/shard_map/all_to_all | solution.py:67
  239.4 1.4 copy.77
  240.8 2.2 all_to_all.59
  243.0 1.8 fusion.26
  244.8 0.0 copy-done.3
  244.9 0.1 copy-done.1
  245.0 0.3 copy-done.2
  245.3 2.6 fusion.12
  247.9 137.5 %reduce-scatter.4.cloned.1.call-done = bf16[64,2048]{1,0:T(8,128)(2,1)} async-done(((bf16[2048,2048]{1,0:T(8,128)(2,1)}), bf16[64,2048]{1,0:T(8,128)(2,1)}) %reduce-scatter.4.cloned.1.call-update) | async-done | bytes 262160
  385.4 2.0 copy.59
  387.3 0.0 all-reduce.2.cloned.1.call-update
  387.4 7.1 %fusion.7 = bf16[1,256,2048]{2,1,0:T(8,128)(2,1)} fusion(bf16[256,2048]{1,0:T(8,128)(2,1)} %get-tuple-element.18, bf16[2048,2048]{1,0:T(8,128)(2,1)} %all-gather.2.cloned.1.call-done), kind=kOutput, calls=%fused_computation.19 | convolution fusion | flops 2148007936 | bytes 10485760 | tf_op jit(solution)/shard_map/tc,ic->ti/dot_general | solution.py:81
  394.4 60.1 %all-reduce.2.cloned.1.call-done = bf16[64,2048]{0,1:T(8,128)(2,1)} async-done(((bf16[64,2048]{0,1:T(8,128)(2,1)}), bf16[64,2048]{0,1:T(8,128)(2,1)}) %all-reduce.2.cloned.1.call-update) | async-done | bytes 262160 | tf_op jit(solution)/shard_map/psum | solution.py:96
  454.5 2.0 copy.52
  (9 shorter events, 0.0 us)
Async XLA Ops:
  7.2 112.1 %copy-start = (bf16[1,256,2048]{2,1,0:T(8,128)(2,1)S(1)}, bf16[1,256,2048]{2,1,0:T(8,128)(2,1)}, u32[]{:S(2)}) copy-start(bf16[1,256,2048]{2,1,0:T(8,128)(2,1)} %param.10) | copy-start | bytes 3145732
  7.2 2.7 copy-start.5
  7.2 133.6 %all-gather.2.cloned.1.call-start = ((), (), s32[]{:S(2)}) async-start(), calls=%async_computation.5 | async-start | bytes 8650752 | tf_op jit(solution)/shard_map/all_gather | solution.py:47
  7.9 377.5 %reduce-scatter.4.cloned.1.call-start = ((), (), s32[]{:S(2)}) async-start(), calls=%async_computation.7 | async-start | bytes 8650752
  14.0 47.3 %copy-start.7 = (bf16[4,64,64]{2,1,0:T(8,128)(2,1)S(1)}, bf16[4,64,64]{2,1,0:T(8,128)(2,1)}, u32[]{:S(2)}) copy-start(bf16[4,64,64]{2,1,0:T(8,128)(2,1)} %param.17) | copy-start | bytes 98308
  14.0 47.3 %copy-start.8 = (bf16[4,64,64]{2,1,0:T(8,128)(2,1)S(1)}, bf16[4,64,64]{2,1,0:T(8,128)(2,1)}, u32[]{:S(2)}) copy-start(bf16[4,64,64]{2,1,0:T(8,128)(2,1)} %param.15) | copy-start | bytes 98308
  59.8 1.5 copy-start.4
  114.6 1.6 copy-start.6
  114.6 1.6 copy-start.9
  137.4 317.1 %all-reduce.2.cloned.1.call-start = ((), (), s32[]{:S(2)}) async-start(), calls=%async_computation.6 | async-start | bytes 1048576 | tf_op jit(solution)/shard_map/psum | solution.py:96
  240.8 4.0 copy-start.3
  243.0 2.0 copy-start.1
  243.0 2.2 copy-start.2
Sparse Core Ops, SparseCore 0:
  10.6 130.1 all-gather.1
  144.8 240.5 reduce-scatter.3
  388.4 66.0 all-reduce.1
where the time goes:
time: 465 us; the launch traced here: 463 us
  waiting for transfers between devices  201 us (43%)
  blocking collectives  173 us (37%)
  matrix products  36.4 us (8%)
  local copies, waits for them, and re-layouts  33.4 us (7%)
  between operations  13.9 us (3%)
    unnamed x4, waiting for transfers between devices  138 us
    psum x1, waiting for transfers between devices, per_device(): grad_weight = lax.psum(partial_rows, 'dp').astype(jnp.float32)  60.1 us
    all_to_all x1, blocking collectives, per_device(): lax.all_to_all(grad_first, 'context', split_axis=0, concat_axis=1, tiled=...  46.2 us
    all_to_all x1, blocking collectives, per_device(): lax.all_to_all(grad_third, 'context', split_axis=1, concat_axis=0, tiled=...  45.7 us
    all_to_all x1, blocking collectives, per_device(): lax.all_to_all(first_mix, 'context', split_axis=1, concat_axis=0, tiled=T...  40.9 us
    all_to_all x1, blocking collectives, per_device(): lax.all_to_all(third_mix, 'context', split_axis=0, concat_axis=1, tiled=T...  40.2 us
    unnamed x23, local copies, waits for them, and re-layouts  16.9 us
  transfers between devices with their start and end apart: 3, of which 3 were waited for; matrix products, arithmetic and copies ran while one was open for 14% of the time, Pallas kernels for 0%

commit v1 on v0

v1 whole, which is shorter than its diff:
```python
import functools

import jax
import jax.numpy as jnp
from jax import lax
from jax.experimental import pallas as pl
from jax.experimental.pallas import tpu as pltpu
from jax.sharding import PartitionSpec as P

BF = jnp.bfloat16
F32 = jnp.float32
MESH = pl.DeviceIdType.MESH
X = 4
NC = 2


def mm(a, b):
    return jnp.dot(a, b, preferred_element_type=F32)


def mm_ta(a, b):
    return lax.dot_general(a, b, (((0,), (0,)), ((), ())), preferred_element_type=F32)


def mm_tb(a, b):
    return lax.dot_general(a, b, (((1,), (1,)), ((), ())), preferred_element_type=F32)


def iota(shape, dim):
    return lax.broadcasted_iota(jnp.int32, shape, dim)


def ones_where(cond):
    return jnp.where(cond, 1.0, 0.0).astype(BF)


def loop(lo, hi, body):
    lax.fori_loop(lo, hi, lambda i, c: (body(i), c)[1], 0)


def kernel(
    Y,
    tok, wgt, gate, skip, f1, f2, kern, f3, f4, cot,
    mixed, gtok, ggate, gwt,
    tother, g, gx, gp, p, wb, gw, sb, rb, rxa, rxc, sx, ry, sy, rz, fin, gfin,
    a1, a2, a3t, a4t, u, gts, gtr, pgs, pgr, pgo,
    s_ag, r_ag, s_pair, r_pair, s_a2a, r_a2a, s_rs, r_rs,
):
    dp = lax.axis_index("dp")
    k = lax.axis_index("context")
    DP = 2 * X
    Z = wb.shape[0]
    CTX = Z * Y
    h, x = lax.rem(dp, 2), lax.div(dp, 2)
    z, y = lax.div(k, Y), lax.rem(k, Y)
    right, left = lax.rem(x + 1, X), lax.rem(x + X - 1, X)
    opp = lax.rem(x + 2, X)
    other = 1 - h
    pair = x * 2 + other
    rows, D = tok.shape
    HC = D // 2
    QL, R = f1.shape[0], f1.shape[1]
    SL, Q = f2.shape[0], f2.shape[1]
    M = 2 * rows
    CH = M // CTX
    CW = HC // NC
    WR = wb.shape[3]
    half = pl.multiple_of(h * HC, HC)
    ohalf = pl.multiple_of(other * HC, HC)
    ZH = Z // 2
    TI = D // Z

    def remote(src, dst, ss, rs, dev):
        return pltpu.make_async_remote_copy(
            src_ref=src, dst_ref=dst, send_sem=ss, recv_sem=rs, device_id=dev, device_id_type=MESH
        )

    EB = 32

    def gate_rows(i):
        r = pl.ds(pl.multiple_of(i * EB, EB), EB)
        g[h, r, :] = (cot[r, pl.ds(half, HC)].astype(F32) * gate[r, pl.ds(half, HC)].astype(F32)).astype(BF)
        gx[r, :] = (cot[r, pl.ds(ohalf, HC)].astype(F32) * gate[r, pl.ds(ohalf, HC)].astype(F32)).astype(BF)

    loop(0, rows // EB, gate_rows)

    barrier = pltpu.get_barrier_semaphore()

    def greet_context(d):
        pl.semaphore_signal(barrier, inc=1, device_id=(dp, lax.rem(k + d, CTX)), device_id_type=MESH)

    def greet_dp(d):
        pl.semaphore_signal(barrier, inc=1, device_id=(lax.rem(dp + d, DP), k), device_id_type=MESH)

    loop(1, CTX, greet_context)
    loop(1, DP, greet_dp)
    pl.semaphore_wait(barrier, CTX - 1 + DP - 1)

    c_g = remote(gx, g.at[h], s_pair.at[0], r_pair.at[0], (pair, k))
    c_g.start()

    def ag_z(d):
        zz = lax.rem(z + d, Z)
        remote(
            wgt.at[x, :, pl.ds(half, HC)], wb.at[z, y, x], s_ag.at[0], r_ag.at[0], (dp, zz * Y + y)
        ).start()

    loop(1, Z, ag_z)
    c_tok = remote(tok, tother, s_pair.at[1], r_pair.at[1], (pair, k))
    c_tok.start()
    wb[z, y, x] = wgt[x, :, pl.ds(half, HC)]

    def row_matrix(dst, factor, transposed):
        rr, ss = iota((M, R), 0), iota((M, R), 1)
        for b in range(2):
            for q in range(QL):
                e = ones_where(rr == (ss // SL) * CH + b * (QL * SL) + q * SL + ss % SL)
                block = mm_tb(e, factor[q]) if transposed else mm(e, factor[q])
                dst[:, (b * QL + q) * R:(b * QL + q + 1) * R] = block.astype(BF)

    def column_matrix(dst, factor, transposed):
        qq, cc = iota((Q, M), 0), iota((Q, M), 1)
        for s in range(SL):
            e = ones_where(
                (cc // CH == qq // QL) & ((cc // SL) % QL == qq % QL) & (cc % SL == s)
            )
            block = mm_ta(factor[s], e) if transposed else mm(factor[s], e)
            u[s * Q:(s + 1) * Q, :] = block.astype(BF)
        rr, cc = iota((Q * SL, SL * Q), 0), iota((Q * SL, SL * Q), 1)
        move = ones_where((rr // SL == cc % Q) & (rr % SL == cc // Q))
        full = mm(move, u[...])
        owner = (iota((Q * SL, M), 1) // (QL * SL)) % 2
        for b in range(2):
            dst[b * Q * SL:(b + 1) * Q * SL, :] = jnp.where(owner == b, full, 0.0).astype(BF)

    row_matrix(a4t, f4, True)
    column_matrix(a3t, f3, True)

    def a2a_start(ph, c):
        def send(d):
            kk = lax.rem(k + d, CTX)
            remote(
                sb.at[ph, c, kk], rb.at[ph, c, k], s_a2a.at[ph, c], r_a2a.at[ph, c], (dp, kk)
            ).start()

        loop(1, CTX, send)
        rb[ph, c, k] = sb[ph, c, k]

    def a2a_desc(ph, c):
        most = pl.ds(0, CTX - 1)
        return remote(
            sb.at[ph, c, most], rb.at[ph, c, most], s_a2a.at[ph, c], r_a2a.at[ph, c],
            (dp, lax.rem(k + 1, CTX)),
        )

    def put(ph, c, value):
        sb[ph, c] = value.astype(BF).reshape(CTX, CH, CW)

    def got(ph, c):
        return rb[ph, c].reshape(M, CW)

    def cols(c):
        return slice(c * CW, (c + 1) * CW)

    c_g.wait_recv()
    for c in range(NC):
        put(0, c, mm(a4t[...], g[:, :, cols(c)].reshape(M, CW)))
        a2a_start(0, c)

    column_matrix(a2, f2, False)

    zs = pl.ds(0, Z - 1)
    remote(wb.at[zs, y, x], wb.at[zs, y, x], s_ag.at[0], r_ag.at[0], (pair, k)).wait_recv()

    def ag_y(d):
        yy = lax.rem(y + d, Y)
        remote(wb.at[:, y, x], wb.at[:, y, x], s_ag.at[1], r_ag.at[1], (dp, z * Y + yy)).start()

    loop(1, Y, ag_y)
    row_matrix(a1, f1, False)
    ys = pl.ds(0, Y - 1)
    ag_y_desc = remote(wb.at[:, ys, x], wb.at[:, ys, x], s_ag.at[1], r_ag.at[1], (pair, k))
    ag_y_desc.wait_recv()
    rdev, ldev = (right * 2 + h, k), (left * 2 + h, k)
    c_xr = remote(wb.at[:, :, x], wb.at[:, :, x], s_ag.at[2], r_ag.at[2], rdev)
    c_xl = remote(wb.at[:, :, x], wb.at[:, :, x], s_ag.at[3], r_ag.at[3], ldev)
    c_xr.start()
    c_xl.start()

    def kern_of(c):
        return kern[:, pl.ds(pl.multiple_of(h * HC + c * CW, CW), CW)].astype(F32)

    def filtered(value, c):
        kc = kern_of(c)
        return (value.reshape(2, Q * SL, CW) * kc[None]).astype(BF).reshape(M, CW)

    for c in range(NC):
        a2a_desc(0, c).wait_recv()
        gs = filtered(mm(a3t[...], got(0, c)), c)
        put(1, c, mm_ta(a2[...], gs))
        a2a_start(1, c)

    lo, hi = pl.ds(0, ZH), pl.ds(ZH, Z - ZH)
    c_xr.wait_recv()
    c_xr2 = remote(wb.at[lo, :, left], wb.at[lo, :, left], s_ag.at[4], r_ag.at[4], rdev)
    c_xr2.start()
    c_xl.wait_recv()
    c_xl2 = remote(wb.at[hi, :, right], wb.at[hi, :, right], s_ag.at[5], r_ag.at[5], ldev)
    c_xl2.start()
    c_tok.wait_recv()
    c_xr2.wait_recv()
    c_xl2.wait_recv()

    for c in range(NC):
        wc = wb[:, :, :, :, cols(c)].reshape(D, CW)
        p[h, :, cols(c)] = mm(tok[...], wc).astype(BF)
        p[other, :, cols(c)] = mm(tother[...], wc).astype(BF)
        put(2, c, mm(a1[...], p[:, :, cols(c)].reshape(M, CW)))
        a2a_start(2, c)

    def skip_of(c):
        return skip[:, pl.ds(pl.multiple_of(h * HC + c * CW, CW), CW)]

    for c in range(NC):
        a2a_desc(1, c).wait_recv()
        gf = mm_ta(a1[...], got(1, c)) + skip_of(c) * g[:, :, cols(c)].reshape(M, CW).astype(F32)
        gp[:, :, cols(c)] = gf.astype(BF).reshape(2, rows, CW)

    def gw_rows(i):
        at = pl.ds(pl.multiple_of(i * TI, TI), TI)
        part = mm_ta(tok[:, at], gp[h]) + mm_ta(tother[:, at], gp[other])
        gw[i] = part.astype(BF).reshape(Y, X, WR, HC)

    loop(0, Z, gw_rows)
    c_r1 = remote(gw.at[lo, :, opp], rxa.at[0], s_rs.at[0], r_rs.at[0], rdev)
    c_l1 = remote(gw.at[hi, :, opp], rxa.at[1], s_rs.at[1], r_rs.at[1], ldev)
    c_r2 = remote(gw.at[hi, :, right], rxc.at[0, hi], s_rs.at[2], r_rs.at[2], rdev)
    c_l2 = remote(gw.at[lo, :, left], rxc.at[1, lo], s_rs.at[3], r_rs.at[3], ldev)
    for copy in (c_r1, c_l1, c_r2, c_l2):
        copy.start()

    for c in range(NC):
        a2a_desc(2, c).wait_recv()
        fl = filtered(mm(a2[...], got(2, c)), c)
        put(3, c, mm_ta(a3t[...], fl))
        a2a_start(3, c)

    c_r1.wait_recv()

    def add_right(i):
        gw[i, :, right] = (gw[i, :, right].astype(F32) + rxa[0, i].astype(F32)).astype(BF)

    loop(0, ZH, add_right)
    c_r3 = remote(gw.at[lo, :, right], rxc.at[0, lo], s_rs.at[4], r_rs.at[4], rdev)
    c_r3.start()
    c_l1.wait_recv()

    def add_left(i):
        gw[ZH + i, :, left] = (gw[ZH + i, :, left].astype(F32) + rxa[1, i].astype(F32)).astype(BF)

    loop(0, ZH, add_left)
    c_l3 = remote(gw.at[hi, :, left], rxc.at[1, hi], s_rs.at[5], r_rs.at[5], ldev)
    c_l3.start()

    def gt_other(i):
        at = pl.ds(pl.multiple_of(i * TI, TI), TI)
        gts[:, at] = mm_tb(gp[other], wb[i].reshape(TI, HC)).astype(BF)

    loop(0, Z, gt_other)
    c_gt = remote(gts, gtr, s_pair.at[2], r_pair.at[2], (pair, k))
    c_gt.start()

    for copy in (c_r2, c_l2, c_r3, c_l3):
        copy.wait_recv()

    def sum_x(i):
        sx[i] = (gw[i, :, x].astype(F32) + rxc[0, i].astype(F32) + rxc[1, i].astype(F32)).astype(BF)

    loop(0, Z, sum_x)

    def rs_y(d):
        yy = lax.rem(y + d, Y)
        remote(sx.at[:, yy], ry.at[d - 1], s_rs.at[6], r_rs.at[6], (dp, z * Y + yy)).start()

    loop(1, Y, rs_y)
    rs_y_desc = remote(ry, ry, s_rs.at[6], r_rs.at[6], (pair, k))

    c_gt.wait_recv()

    def gt_own(i):
        at = pl.ds(pl.multiple_of(i * TI, TI), TI)
        gtok[:, at] = (mm_tb(gp[h], wb[i].reshape(TI, HC)) + gtr[:, at].astype(F32)).astype(BF)

    loop(0, Z, gt_own)

    rs_y_desc.wait_recv()

    def sum_y(i):
        total = sx[i, y].astype(F32)
        for d in range(Y - 1):
            total = total + ry[d, i].astype(F32)
        sy[i] = total.astype(BF)

    loop(0, Z, sum_y)

    def rs_z(d):
        zz = lax.rem(z + d, Z)
        remote(sy.at[zz], rz.at[d - 1], s_rs.at[7], r_rs.at[7], (dp, zz * Y + y)).start()

    loop(1, Z, rs_z)

    for c in range(NC):
        a2a_desc(3, c).wait_recv()
        pre = mm_ta(a4t[...], got(3, c)) + skip_of(c) * p[:, :, cols(c)].reshape(M, CW).astype(F32)
        pgo[:, :, cols(c)] = pre.astype(BF).reshape(2, rows, CW)
    c_pg = remote(pgo.at[other], pgr, s_pair.at[3], r_pair.at[3], (pair, k))
    c_pg.start()

    rs_z_desc = remote(rz, rz, s_rs.at[7], r_rs.at[7], (pair, k))
    rs_z_desc.wait_recv()
    total = sy[z].astype(F32)
    for d in range(Z - 1):
        total = total + rz[d].astype(F32)
    fin[...] = total.astype(BF)

    def share(d):
        remote(
            fin, gfin.at[dp], s_rs.at[8], r_rs.at[8], (lax.rem(dp + d, DP), k)
        ).start()

    loop(1, DP, share)
    gfin[dp] = fin[...]

    def gate_out(i):
        r = pl.ds(pl.multiple_of(i * EB, EB), EB)
        own = pgo[h, r, :].astype(F32)
        mixed[r, pl.ds(half, HC)] = (gate[r, pl.ds(half, HC)].astype(F32) * own).astype(BF)
        ggate[r, pl.ds(half, HC)] = (cot[r, pl.ds(half, HC)].astype(F32) * own).astype(BF)

    loop(0, rows // EB, gate_out)
    c_pg.wait_recv()

    def gate_out_other(i):
        r = pl.ds(pl.multiple_of(i * EB, EB), EB)
        got_pre = pgr[r, :].astype(F32)
        mixed[r, pl.ds(ohalf, HC)] = (gate[r, pl.ds(ohalf, HC)].astype(F32) * got_pre).astype(BF)
        ggate[r, pl.ds(ohalf, HC)] = (cot[r, pl.ds(ohalf, HC)].astype(F32) * got_pre).astype(BF)

    loop(0, rows // EB, gate_out_other)

    most = pl.ds(0, DP - 1)
    share_desc = remote(gfin.at[most], gfin.at[most], s_rs.at[8], r_rs.at[8], (pair, k))
    share_desc.wait_recv()
    for j in range(DP):
        xx, hh = j // 2, j % 2
        gwt[xx, :, hh * HC:(hh + 1) * HC] = gfin[j].astype(F32)

    for copy in (c_g, c_tok, c_gt, c_pg, c_xr, c_xl, c_xr2, c_xl2):
        copy.wait_send()
    for copy in (c_r1, c_l1, c_r2, c_l2, c_r3, c_l3):
        copy.wait_send()
    remote(wb.at[zs, y, x], wb.at[zs, y, x], s_ag.at[0], r_ag.at[0], (pair, k)).wait_send()
    ag_y_desc.wait_send()
    rs_y_desc.wait_send()
    rs_z_desc.wait_send()
    share_desc.wait_send()
    for ph in range(4):
        for c in range(NC):
            a2a_desc(ph, c).wait_send()


def per_device(Y, CTX, tokens, weight, gate, skip, first, second, kern, third, fourth, cotangent):
    _, rows, D = tokens.shape
    HC = D // 2
    CW = HC // NC
    Z = CTX // Y
    M = 2 * rows
    CH = M // CTX
    R = first.shape[1]
    SL, Q = second.shape[0], second.shape[1]
    WR = D // CTX // X
    vm = pl.BlockSpec(memory_space=pltpu.VMEM)
    out = pl.pallas_call(
        functools.partial(kernel, Y),
        out_shape=(
            jax.ShapeDtypeStruct((rows, D), BF),
            jax.ShapeDtypeStruct((rows, D), BF),
            jax.ShapeDtypeStruct((rows, D), BF),
            jax.ShapeDtypeStruct((X, WR, D), F32),
        ),
        in_specs=[vm] * 10,
        out_specs=(vm,) * 4,
        scratch_shapes=[
            pltpu.VMEM((rows, D), BF),
            pltpu.VMEM((2, rows, HC), BF),
            pltpu.VMEM((rows, HC), BF),
            pltpu.VMEM((2, rows, HC), BF),
            pltpu.VMEM((2, rows, HC), BF),
            pltpu.VMEM((Z, Y, X, WR, HC), BF),
            pltpu.VMEM((Z, Y, X, WR, HC), BF),
            pltpu.VMEM((4, NC, CTX, CH, CW), BF),
            pltpu.VMEM((4, NC, CTX, CH, CW), BF),
            pltpu.VMEM((2, Z // 2, Y, WR, HC), BF),
            pltpu.VMEM((2, Z, Y, WR, HC), BF),
            pltpu.VMEM((Z, Y, WR, HC), BF),
            pltpu.VMEM((Y - 1, Z, WR, HC), BF),
            pltpu.VMEM((Z, WR, HC), BF),
            pltpu.VMEM((Z - 1, WR, HC), BF),
            pltpu.VMEM((WR, HC), BF),
            pltpu.VMEM((2 * X, WR, HC), BF),
            pltpu.VMEM((M, M), BF),
            pltpu.VMEM((M, M), BF),
            pltpu.VMEM((M, M), BF),
            pltpu.VMEM((M, M), BF),
            pltpu.VMEM((SL * Q, M), BF),
            pltpu.VMEM((rows, D), BF),
            pltpu.VMEM((rows, D), BF),
            pltpu.VMEM((rows, HC), BF),
            pltpu.VMEM((rows, HC), BF),
            pltpu.VMEM((2, rows, HC), BF),
            pltpu.SemaphoreType.DMA((6,)),
            pltpu.SemaphoreType.DMA((6,)),
            pltpu.SemaphoreType.DMA((4,)),
            pltpu.SemaphoreType.DMA((4,)),
            pltpu.SemaphoreType.DMA((4, NC)),
            pltpu.SemaphoreType.DMA((4, NC)),
            pltpu.SemaphoreType.DMA((9,)),
            pltpu.SemaphoreType.DMA((9,)),
        ],
        compiler_params=pltpu.CompilerParams(
            collective_id=0, has_side_effects=True, vmem_limit_bytes=60 * 1024 * 1024
        ),
        cost_estimate=pl.CostEstimate(
            flops=8 * rows * D * D, bytes_accessed=8 * rows * D * 2, transcendentals=0
        ),
    )(
        tokens[0],
        weight.reshape(X, WR, D),
        gate[0],
        skip.reshape(1, D),
        first,
        second,
        kern.reshape(Q * SL, D),
        third,
        fourth,
        cotangent[0],
    )
    mixed, gtok, ggate, gwt = out
    return mixed[None], gtok[None], ggate[None], gwt.reshape(X * WR, D)


def solution(mesh, y_size=4):
    in_specs = (
        P("dp", "context", None),
        P("context", None),
        P("dp", "context", None),
        P(),
        P("context", None, None),
        P("context", None, None),
        P(None, "context", None),
        P("context", None, None),
        P("context", None, None),
        P("dp", "context", None),
    )
    out_specs = (
        P("dp", "context", None),
        P("dp", "context", None),
        P("dp", "context", None),
        P("context", None),
    )
    return jax.shard_map(
        functools.partial(per_device, y_size, mesh.shape["context"]),
        mesh=mesh, in_specs=in_specs, out_specs=out_specs, check_vma=False,
    )
```

time: 465 us -> 158 us (0.34)
  waiting for transfers between devices: 201 us -> 0 us
  blocking collectives: 173 us -> 0 us
  Pallas kernels: 0 us -> 148 us
  matrix products: 36.4 us -> 0 us
  local copies, waits for them, and re-layouts: 33.4 us -> 8.32 us
  between operations: 13.9 us -> 0.65 us
    all_to_all x4 -> x0, blocking collectives: 173 us -> none  [the longest x1 46.2 us: per_device(): lax.all_to_all(grad_first, 'context', split_axis=0, concat_axis=1, tiled=...]
    pallas_call x0 -> x1, Pallas kernels: none -> 148 us  [per_device(): pl.pallas_call(functools.partial(kernel, Y), out_shape=(jax.ShapeDtypeStr...]
    unnamed x4 -> x0, waiting for transfers between devices: 138 us -> none
    psum x1 -> x0, waiting for transfers between devices: 60.1 us -> none  [per_device(): grad_weight = lax.psum(partial_rows, 'dp').astype(jnp.float32)]
    dot_general x9 -> x0, matrix products: 36.4 us -> none  [the longest x1 7.05 us: per_device(): jnp.einsum('tc,ic->ti', grad_proj, lax.all_gather(weight, 'context', axis...]
    unnamed x23 -> x10, local copies, waits for them, and re-layouts: 16.9 us -> 6.19 us
    convert_element_type x4 -> x0, local copies, waits for them, and re-layouts: 9.24 us -> none  [the longest x1 2.58 us: per_device(): first_mix = jnp.einsum('qsr,qrc->qsc', first_factor, proj_blocks, preferr...]
    all_to_all x6 -> x0, local copies, waits for them, and re-layouts: 7.28 us -> none  [the longest x2 3.66 us: per_device(): lax.all_to_all(third_mix, 'context', split_axis=0, concat_axis=1, tiled=T...]
  transfers between devices with their start and end apart: 3 -> 0, of which waited for: 3 -> 0; matrix products, arithmetic and copies ran while one was open for 14% -> 0% of each run, Pallas kernels for 0% -> 0%
where the time goes in v1:
time: 158 us; the launch traced here: 157 us
  Pallas kernels  148 us (94%)
  local copies, waits for them, and re-layouts  8.32 us (5%)
    pallas_call x1, Pallas kernels, per_device(): pl.pallas_call(functools.partial(kernel, Y), out_shape=(jax.ShapeDtypeStr...  148 us
    unnamed x10, local copies, waits for them, and re-layouts  6.19 us

profile of v1, /device:TPU:1, one launch (start us, length us, event | category | flops | bytes accessed | tf_op | source)
XLA Modules:
  0.0 157.1 jit_solution(11195014260399172290)
XLA Ops:
  0.6 2.1 %reshape.22.kern = bf16[256,2048]{1,0:T(8,128)(2,1)} reshape(bf16[64,4,2048]{2,1,0:T(4,128)(2,1)} %param.16) | data formatting | bytes 2097152 | tf_op jit(solution)/shard_map/reshape | solution.py:443
  2.8 148.1 %shard_map.129 = (bf16[256,2048]{1,0:T(8,128)(2,1)}, bf16[256,2048]{1,0:T(8,128)(2,1)}, bf16[256,2048]{1,0:T(8,128)(2,1)}, f32[4,16,2048]{2,1,0:T(8,128)}) custom-call(bf16[256,2048]{1,0:T(8,128)(2,1)} %bitcast.13, bf16[4,16,2048]{2,1,0:T(8,128)(2,1)} %bitcast.16, bf16[256,2048]{1,0:T(8,128)(2,1)} %bitcast.14, f32[1,2048]{1,0:T(1,128)} %bitcast.17, ...), custom_call_target="tpu_custom_call" | custom-call | flops 8589934592 | bytes 8388608 | tf_op jit(solution)/shard_map/pallas_call | solution.py:383
  150.9 0.0 copy-start.1
  150.9 2.4 %copy.18 = bf16[1,256,2048]{2,1,0:T(8,128)(2,1)} copy(bf16[1,256,2048]{2,1,0:T(8,128)(2,1)} %bitcast.11) | data formatting | bytes 2097152
  153.3 0.0 copy-done.1
  153.3 0.0 copy-start
  153.3 1.0 copy.19
  154.3 0.6 copy-done
  154.9 0.0 copy-start.2
  154.9 1.0 copy.20
  155.9 0.4 copy-done.2
  156.3 0.8 copy.21
Async XLA Ops:
  150.9 2.4 %copy-start.1 = (bf16[256,2048]{1,0:T(8,128)(2,1)S(1)}, bf16[256,2048]{1,0:T(8,128)(2,1)}, u32[]{:S(2)}) copy-start(bf16[256,2048]{1,0:T(8,128)(2,1)} %get-tuple-element.9) | copy-start | bytes 3145732
  153.3 1.6 %copy-start = (bf16[256,2048]{1,0:T(8,128)(2,1)S(1)}, bf16[256,2048]{1,0:T(8,128)(2,1)}, u32[]{:S(2)}) copy-start(bf16[256,2048]{1,0:T(8,128)(2,1)} %get-tuple-element.10) | copy-start | bytes 3145732
  154.9 1.4 copy-start.2

commit v2 on v1

v2 whole, which is shorter than its diff:
```python
import functools

import jax
import jax.numpy as jnp
from jax import lax
from jax.experimental import pallas as pl
from jax.experimental.pallas import tpu as pltpu
from jax.sharding import PartitionSpec as P

BF = jnp.bfloat16
F32 = jnp.float32
MESH = pl.DeviceIdType.MESH
X = 4
NC = 2


def mm(a, b):
    return jnp.dot(a, b, preferred_element_type=F32)


def mm_ta(a, b):
    return lax.dot_general(a, b, (((0,), (0,)), ((), ())), preferred_element_type=F32)


def mm_tb(a, b):
    return lax.dot_general(a, b, (((1,), (1,)), ((), ())), preferred_element_type=F32)


def iota(shape, dim):
    return lax.broadcasted_iota(jnp.int32, shape, dim)


def ones_where(cond):
    return jnp.where(cond, 1.0, 0.0).astype(BF)


def loop(lo, hi, body):
    lax.fori_loop(lo, hi, lambda i, c: (body(i), c)[1], 0)


def kernel(
    Y,
    tok, wgt, gate, skip, f1, f2, kern, f3, f4, cot,
    pre, gtown, gtr, gfin,
    tk, tother, gv, cv, kv, g, gx, gp, p, wb, gw, sb, rb, rxa, rxc, sx, ry, sy, rz, fin,
    a1, a2, a3t, a4t, u, gts, gto, pgo,
    s_ag, r_ag, s_pair, r_pair, s_a2a, r_a2a, s_rs, r_rs, s_loc,
):
    dp = lax.axis_index("dp")
    k = lax.axis_index("context")
    DP = 2 * X
    Z = wb.shape[1]
    CTX = Z * Y
    h, x = lax.rem(dp, 2), lax.div(dp, 2)
    z, y = lax.div(k, Y), lax.rem(k, Y)
    right, left = lax.rem(x + 1, X), lax.rem(x + X - 1, X)
    opp = lax.rem(x + 2, X)
    other = 1 - h
    pair = x * 2 + other
    rows, D = tok.shape
    HC = D // 2
    QL, R = f1.shape[0], f1.shape[1]
    SL, Q = f2.shape[0], f2.shape[1]
    M = 2 * rows
    CH = M // CTX
    CW = HC // NC
    WR = wb.shape[4]
    half = pl.multiple_of(h * HC, HC)
    ohalf = pl.multiple_of(other * HC, HC)
    ZH = Z // 2
    TI = D // Z
    rdev, ldev, pdev = (right * 2 + h, k), (left * 2 + h, k), (pair, k)

    def remote(src, dst, ss, rs, dev):
        return pltpu.make_async_remote_copy(
            src_ref=src, dst_ref=dst, send_sem=ss, recv_sem=rs, device_id=dev, device_id_type=MESH
        )

    def local(src, dst, i):
        return pltpu.make_async_copy(src, dst, s_loc.at[i])

    def mine(c):
        return pl.ds(pl.multiple_of(h * HC + c * CW, CW), CW)

    def others(c):
        return pl.ds(pl.multiple_of(other * HC + c * CW, CW), CW)

    in_gate, in_cot = local(gate, gv, 0), local(cot, cv, 1)
    in_kern = local(kern.at[:, :, pl.ds(half, HC)], kv, 2)
    in_tok = local(tok, tk, 3)
    in_w = [local(wgt.at[x, :, mine(c)], wb.at[c, z, y, x], 4 + c) for c in range(NC)]
    in_gate.start()
    in_cot.start()

    barrier = pltpu.get_barrier_semaphore()

    def greet_context(d):
        pl.semaphore_signal(barrier, inc=1, device_id=(dp, lax.rem(k + d, CTX)), device_id_type=MESH)

    def greet_dp(d):
        pl.semaphore_signal(barrier, inc=1, device_id=(lax.rem(dp + d, DP), k), device_id_type=MESH)

    loop(1, DP, greet_dp)
    loop(1, CTX, greet_context)
    for copy in in_w:
        copy.start()
    in_kern.start()
    in_tok.start()

    EB = 32
    in_gate.wait()
    in_cot.wait()

    def gate_rows(i):
        r = pl.ds(pl.multiple_of(i * EB, EB), EB)
        for c in range(NC):
            g[c, h, r, :] = (cv[r, mine(c)].astype(F32) * gv[r, mine(c)].astype(F32)).astype(BF)
            gx[c, r, :] = (cv[r, others(c)].astype(F32) * gv[r, others(c)].astype(F32)).astype(BF)

    loop(0, rows // EB, gate_rows)
    pl.semaphore_wait(barrier, CTX - 1 + DP - 1)

    c_g = [remote(gx.at[c], g.at[c, h], s_pair.at[c], r_pair.at[c], pdev) for c in range(NC)]
    for copy in c_g:
        copy.start()

    def ag_z(c):
        def send(d):
            zz = lax.rem(z + d, Z)
            remote(
                wgt.at[x, :, mine(c)], wb.at[c, z, y, x], s_ag.at[0, c], r_ag.at[0, c], (dp, zz * Y + y)
            ).start()

        loop(1, Z, send)

    def ag_z_desc(c):
        zs = pl.ds(0, Z - 1)
        return remote(wb.at[c, zs, y, x], wb.at[c, zs, y, x], s_ag.at[0, c], r_ag.at[0, c], pdev)

    for c in range(NC):
        ag_z(c)

    def row_matrix(dst, factor, transposed):
        rr, ss = iota((M, R), 0), iota((M, R), 1)
        for b in range(2):
            for q in range(QL):
                e = ones_where(rr == (ss // SL) * CH + b * (QL * SL) + q * SL + ss % SL)
                block = mm_tb(e, factor[q]) if transposed else mm(e, factor[q])
                dst[:, (b * QL + q) * R:(b * QL + q + 1) * R] = block.astype(BF)

    def column_matrix(dst, factor, transposed):
        qq, cc = iota((Q, M), 0), iota((Q, M), 1)
        for s in range(SL):
            e = ones_where(
                (cc // CH == qq // QL) & ((cc // SL) % QL == qq % QL) & (cc % SL == s)
            )
            block = mm_ta(factor[s], e) if transposed else mm(factor[s], e)
            u[s * Q:(s + 1) * Q, :] = block.astype(BF)
        rr, cc = iota((Q * SL, SL * Q), 0), iota((Q * SL, SL * Q), 1)
        move = ones_where((rr // SL == cc % Q) & (rr % SL == cc // Q))
        full = mm(move, u[...])
        owner = (iota((Q * SL, M), 1) // (QL * SL)) % 2
        for b in range(2):
            dst[b * Q * SL:(b + 1) * Q * SL, :] = jnp.where(owner == b, full, 0.0).astype(BF)

    def a2a_start(ph, c):
        def send(d):
            kk = lax.rem(k + d, CTX)
            remote(
                sb.at[ph, c, kk], rb.at[ph, c, k], s_a2a.at[ph, c], r_a2a.at[ph, c], (dp, kk)
            ).start()

        loop(1, CTX, send)
        rb[ph, c, k] = sb[ph, c, k]

    def a2a_desc(ph, c):
        most = pl.ds(0, CTX - 1)
        return remote(
            sb.at[ph, c, most], rb.at[ph, c, most], s_a2a.at[ph, c], r_a2a.at[ph, c],
            (dp, lax.rem(k + 1, CTX)),
        )

    def put(ph, c, value):
        sb[ph, c] = value.astype(BF).reshape(CTX, CH, CW)

    def got(ph, c):
        return rb[ph, c].reshape(M, CW)

    def cols(c):
        return slice(c * CW, (c + 1) * CW)

    row_matrix(a4t, f4, True)

    for c in range(NC):
        c_g[c].wait_recv()
        put(0, c, mm(a4t[...], g[c].reshape(M, CW)))
        a2a_start(0, c)

    def ag_y(c):
        ag_z_desc(c).wait_recv()
        in_w[c].wait()

        def send(d):
            yy = lax.rem(y + d, Y)
            remote(
                wb.at[c, :, y, x], wb.at[c, :, y, x], s_ag.at[1, c], r_ag.at[1, c], (dp, z * Y + yy)
            ).start()

        loop(1, Y, send)

    def ag_y_desc(c):
        ys = pl.ds(0, Y - 1)
        return remote(wb.at[c, :, ys, x], wb.at[c, :, ys, x], s_ag.at[1, c], r_ag.at[1, c], pdev)

    for c in range(NC):
        ag_y(c)
    c_tok = remote(tok, tother, s_pair.at[NC], r_pair.at[NC], pdev)
    c_tok.start()
    column_matrix(a3t, f3, True)

    lo, hi = pl.ds(0, ZH), pl.ds(ZH, Z - ZH)
    c_xr = [remote(wb.at[c, :, :, x], wb.at[c, :, :, x], s_ag.at[2, c], r_ag.at[2, c], rdev) for c in range(NC)]
    c_xl = [remote(wb.at[c, :, :, x], wb.at[c, :, :, x], s_ag.at[3, c], r_ag.at[3, c], ldev) for c in range(NC)]
    c_xr2 = [remote(wb.at[c, lo, :, left], wb.at[c, lo, :, left], s_ag.at[4, c], r_ag.at[4, c], rdev) for c in range(NC)]
    c_xl2 = [remote(wb.at[c, hi, :, right], wb.at[c, hi, :, right], s_ag.at[5, c], r_ag.at[5, c], ldev) for c in range(NC)]

    def ag_x1(c):
        ag_y_desc(c).wait_recv()
        c_xr[c].start()
        c_xl[c].start()

    def ag_x2(c):
        c_xr[c].wait_recv()
        c_xr2[c].start()
        c_xl[c].wait_recv()
        c_xl2[c].start()

    ag_x1(0)
    column_matrix(a2, f2, False)
    for c in range(1, NC):
        ag_x1(c)
    row_matrix(a1, f1, False)

    def filtered(value, c):
        kc = kv[:, :, cols(c)].astype(F32).reshape(Q * SL, CW)
        return (value.reshape(2, Q * SL, CW) * kc[None]).astype(BF).reshape(M, CW)

    def back_columns(c):
        a2a_desc(0, c).wait_recv()
        gs = filtered(mm(a3t[...], got(0, c)), c)
        put(1, c, mm_ta(a2[...], gs))
        a2a_start(1, c)

    def forward_columns(c):
        a2a_desc(2, c).wait_recv()
        fl = filtered(mm(a2[...], got(2, c)), c)
        put(3, c, mm_ta(a3t[...], fl))
        a2a_start(3, c)

    def project(c):
        c_xr2[c].wait_recv()
        c_xl2[c].wait_recv()
        wc = wb[c].reshape(D, CW)
        p[c, h] = mm(tk[...], wc).astype(BF)
        p[c, other] = mm(tother[...], wc).astype(BF)
        put(2, c, mm(a1[...], p[c].reshape(M, CW)))

    def gradient_rows(c):
        gf = mm_ta(a1[...], got(1, c)) + skip[:, mine(c)] * g[c].reshape(M, CW).astype(F32)
        gp[c] = gf.astype(BF).reshape(2, rows, CW)

    def rs_copies(c):
        return (
            remote(gw.at[c, lo, :, opp], rxa.at[c, 0], s_rs.at[0, c], r_rs.at[0, c], rdev),
            remote(gw.at[c, hi, :, opp], rxa.at[c, 1], s_rs.at[1, c], r_rs.at[1, c], ldev),
            remote(gw.at[c, hi, :, right], rxc.at[c, 0, hi], s_rs.at[2, c], r_rs.at[2, c], rdev),
            remote(gw.at[c, lo, :, left], rxc.at[c, 1, lo], s_rs.at[3, c], r_rs.at[3, c], ldev),
            remote(gw.at[c, lo, :, right], rxc.at[c, 0, lo], s_rs.at[4, c], r_rs.at[4, c], rdev),
            remote(gw.at[c, hi, :, left], rxc.at[c, 1, hi], s_rs.at[5, c], r_rs.at[5, c], ldev),
        )

    def rs_x1(c):
        def part_rows(i):
            at = pl.ds(pl.multiple_of(i * TI, TI), TI)
            part = mm_ta(tk[:, at], gp[c, h]) + mm_ta(tother[:, at], gp[c, other])
            gw[c, i] = part.astype(BF).reshape(Y, X, WR, CW)

        loop(0, Z, part_rows)
        for copy in rs_copies(c)[:4]:
            copy.start()

    def rs_x2(c):
        copies = rs_copies(c)

        def add_right(i):
            gw[c, i, :, right] = (gw[c, i, :, right].astype(F32) + rxa[c, 0, i].astype(F32)).astype(BF)

        def add_left(i):
            gw[c, ZH + i, :, left] = (
                gw[c, ZH + i, :, left].astype(F32) + rxa[c, 1, i].astype(F32)
            ).astype(BF)

        copies[0].wait_recv()
        loop(0, ZH, add_right)
        copies[4].start()
        copies[1].wait_recv()
        loop(0, ZH, add_left)
        copies[5].start()

    def rs_y(c):
        for copy in rs_copies(c)[2:]:
            copy.wait_recv()

        def sum_x(i):
            sx[c, i] = (
                gw[c, i, :, x].astype(F32) + rxc[c, 0, i].astype(F32) + rxc[c, 1, i].astype(F32)
            ).astype(BF)

        loop(0, Z, sum_x)

        def send(d):
            yy = lax.rem(y + d, Y)
            remote(
                sx.at[c, :, yy], ry.at[c, d - 1], s_rs.at[6, c], r_rs.at[6, c], (dp, z * Y + yy)
            ).start()

        loop(1, Y, send)

    def rs_y_desc(c):
        return remote(ry.at[c], ry.at[c], s_rs.at[6, c], r_rs.at[6, c], pdev)

    def rs_z(c):
        rs_y_desc(c).wait_recv()

        def sum_y(i):
            total = sx[c, i, y].astype(F32)
            for d in range(Y - 1):
                total = total + ry[c, d, i].astype(F32)
            sy[c, i] = total.astype(BF)

        loop(0, Z, sum_y)

        def send(d):
            zz = lax.rem(z + d, Z)
            remote(
                sy.at[c, zz], rz.at[c, d - 1], s_rs.at[7, c], r_rs.at[7, c], (dp, zz * Y + y)
            ).start()

        loop(1, Z, send)

    def rs_z_desc(c):
        return remote(rz.at[c], rz.at[c], s_rs.at[7, c], r_rs.at[7, c], pdev)

    def rs_sum(c):
        rs_z_desc(c).wait_recv()
        total = sy[c, z].astype(F32)
        for d in range(Z - 1):
            total = total + rz[c, d].astype(F32)
        fin[:, cols(c)] = total.astype(BF)

    def field_rows(c):
        a2a_desc(3, c).wait_recv()
        front = mm_ta(a4t[...], got(3, c)) + skip[:, mine(c)] * p[c].reshape(M, CW).astype(F32)
        pgo[c] = front.astype(BF).reshape(2, rows, CW)

    out_pre = [local(pgo.at[c, h], pre.at[:, mine(c)], 4 + NC + c) for c in range(NC)]
    c_pre = [
        remote(pgo.at[c, other], pre.at[:, mine(c)], s_pair.at[NC + 2 + c], r_pair.at[NC + 2 + c], pdev)
        for c in range(NC)
    ]

    in_kern.wait()
    back_columns(0)
    ag_x2(0)
    for c in range(1, NC):
        back_columns(c)
        ag_x2(c)
    in_tok.wait()
    c_tok.wait_recv()
    project(0)

    a2a_desc(1, 0).wait_recv()
    a2a_start(2, 0)
    gradient_rows(0)
    rs_x1(0)
    for c in range(1, NC):
        project(c)
        rs_x2(c - 1)
        a2a_desc(1, c).wait_recv()
        a2a_start(2, c)
        gradient_rows(c)
        rs_x1(c)

    def token_rows(i, b):
        total = mm_tb(gp[0, b], wb[0, i].reshape(TI, CW))
        for c in range(1, NC):
            total = total + mm_tb(gp[c, b], wb[c, i].reshape(TI, CW))
        return total.astype(BF)

    def gt_other(i):
        gts[:, pl.ds(pl.multiple_of(i * TI, TI), TI)] = token_rows(i, other)

    loop(0, Z, gt_other)
    c_gt = remote(gts, gtr, s_pair.at[NC + 1], r_pair.at[NC + 1], pdev)
    c_gt.start()

    forward_columns(0)
    rs_x2(NC - 1)
    rs_y(0)
    for c in range(1, NC):
        forward_columns(c)
        rs_z(c - 1)
        rs_y(c)

    def gt_own(i):
        gto[:, pl.ds(pl.multiple_of(i * TI, TI), TI)] = token_rows(i, h)

    loop(0, Z, gt_own)
    out_gt = local(gto, gtown, 4 + 2 * NC)
    out_gt.start()

    for c in range(NC - 1):
        rs_sum(c)
        field_rows(c)
        out_pre[c].start()
        c_pre[c].start()
    rs_z(NC - 1)
    rs_sum(NC - 1)
    my_rows = gfin.at[dp]

    def share(d):
        remote(fin, my_rows, s_rs.at[8, 0], r_rs.at[8, 0], (lax.rem(dp + d, DP), k)).start()

    loop(1, DP, share)
    out_fin = local(fin, my_rows, 5 + 2 * NC)
    out_fin.start()
    field_rows(NC - 1)
    out_pre[NC - 1].start()
    c_pre[NC - 1].start()
    share_desc = remote(
        gfin.at[pl.ds(0, DP - 1)], gfin.at[pl.ds(0, DP - 1)], s_rs.at[8, 0], r_rs.at[8, 0], pdev
    )

    for c in range(NC):
        out_pre[c].wait()
        c_pre[c].wait()
        c_g[c].wait_send()
        for copy in (c_xr[c], c_xl[c], c_xr2[c], c_xl2[c], ag_z_desc(c), ag_y_desc(c)):
            copy.wait_send()
        for copy in rs_copies(c):
            copy.wait_send()
        rs_y_desc(c).wait_send()
        rs_z_desc(c).wait_send()
        for ph in range(4):
            a2a_desc(ph, c).wait_send()
    c_tok.wait_send()
    c_gt.wait()
    out_gt.wait()
    out_fin.wait()
    share_desc.wait()


def finish(pre, gate, cot, gtown, gtr, gfin, mixed, gtok, ggate, gwt):
    front = pre[...].astype(F32)
    mixed[...] = (gate[...].astype(F32) * front).astype(BF)
    ggate[...] = (cot[...].astype(F32) * front).astype(BF)
    gtok[...] = (gtown[...].astype(F32) + gtr[...].astype(F32)).astype(BF)
    HC = gfin.shape[2]
    for j in range(2):
        gwt[0, :, j * HC:(j + 1) * HC] = gfin[j].astype(F32)


def per_device(Y, CTX, tokens, weight, gate, skip, first, second, kern, third, fourth, cotangent):
    _, rows, D = tokens.shape
    HC = D // 2
    CW = HC // NC
    Z = CTX // Y
    M = 2 * rows
    CH = M // CTX
    R = first.shape[1]
    SL, Q = second.shape[0], second.shape[1]
    WR = D // CTX // X
    vm = pl.BlockSpec(memory_space=pltpu.VMEM)
    hbm = pl.BlockSpec(memory_space=pl.ANY)
    pre, gtown, gtr, gfin = pl.pallas_call(
        functools.partial(kernel, Y),
        out_shape=(
            jax.ShapeDtypeStruct((rows, D), BF),
            jax.ShapeDtypeStruct((rows, D), BF),
            jax.ShapeDtypeStruct((rows, D), BF),
            jax.ShapeDtypeStruct((2 * X, WR, HC), BF),
        ),
        in_specs=[hbm, hbm, hbm, vm, vm, vm, hbm, vm, vm, hbm],
        out_specs=(hbm,) * 4,
        scratch_shapes=[
            pltpu.VMEM((rows, D), BF),
            pltpu.VMEM((rows, D), BF),
            pltpu.VMEM((rows, D), BF),
            pltpu.VMEM((rows, D), BF),
            pltpu.VMEM((Q, SL, HC), BF),
            pltpu.VMEM((NC, 2, rows, CW), BF),
            pltpu.VMEM((NC, rows, CW), BF),
            pltpu.VMEM((NC, 2, rows, CW), BF),
            pltpu.VMEM((NC, 2, rows, CW), BF),
            pltpu.VMEM((NC, Z, Y, X, WR, CW), BF),
            pltpu.VMEM((NC, Z, Y, X, WR, CW), BF),
            pltpu.VMEM((4, NC, CTX, CH, CW), BF),
            pltpu.VMEM((4, NC, CTX, CH, CW), BF),
            pltpu.VMEM((NC, 2, Z // 2, Y, WR, CW), BF),
            pltpu.VMEM((NC, 2, Z, Y, WR, CW), BF),
            pltpu.VMEM((NC, Z, Y, WR, CW), BF),
            pltpu.VMEM((NC, Y - 1, Z, WR, CW), BF),
            pltpu.VMEM((NC, Z, WR, CW), BF),
            pltpu.VMEM((NC, Z - 1, WR, CW), BF),
            pltpu.VMEM((WR, HC), BF),
            pltpu.VMEM((M, M), BF),
            pltpu.VMEM((M, M), BF),
            pltpu.VMEM((M, M), BF),
            pltpu.VMEM((M, M), BF),
            pltpu.VMEM((SL * Q, M), BF),
            pltpu.VMEM((rows, D), BF),
            pltpu.VMEM((rows, D), BF),
            pltpu.VMEM((NC, 2, rows, CW), BF),
            pltpu.SemaphoreType.DMA((6, NC)),
            pltpu.SemaphoreType.DMA((6, NC)),
            pltpu.SemaphoreType.DMA((2 * NC + 2,)),
            pltpu.SemaphoreType.DMA((2 * NC + 2,)),
            pltpu.SemaphoreType.DMA((4, NC)),
            pltpu.SemaphoreType.DMA((4, NC)),
            pltpu.SemaphoreType.DMA((9, NC)),
            pltpu.SemaphoreType.DMA((9, NC)),
            pltpu.SemaphoreType.DMA((2 * NC + 6,)),
        ],
        compiler_params=pltpu.CompilerParams(
            collective_id=0, has_side_effects=True, vmem_limit_bytes=60 * 1024 * 1024
        ),
        cost_estimate=pl.CostEstimate(
            flops=8 * rows * D * D, bytes_accessed=8 * rows * D * 2, transcendentals=0
        ),
    )(
        tokens[0],
        weight.reshape(X, WR, D),
        gate[0],
        skip.reshape(1, D),
        first,
        second,
        kern,
        third,
        fourth,
        cotangent[0],
    )
    block = pl.BlockSpec((rows // X, D), lambda i: (i, 0))
    wide = pl.BlockSpec((1, WR, D), lambda i: (i, 0, 0))
    two = pl.BlockSpec((2, WR, HC), lambda i: (i, 0, 0))
    mixed, gtok, ggate, gwt = pl.pallas_call(
        finish,
        grid=(X,),
        out_shape=(
            jax.ShapeDtypeStruct((rows, D), BF),
            jax.ShapeDtypeStruct((rows, D), BF),
            jax.ShapeDtypeStruct((rows, D), BF),
            jax.ShapeDtypeStruct((X, WR, D), F32),
        ),
        in_specs=[block, block, block, block, block, two],
        out_specs=(block, block, block, wide),
        compiler_params=pltpu.CompilerParams(vmem_limit_bytes=16 * 1024 * 1024),
        cost_estimate=pl.CostEstimate(
            flops=8 * rows * D, bytes_accessed=16 * rows * D, transcendentals=0
        ),
    )(pre, gate[0], cotangent[0], gtown, gtr, gfin)
    return mixed[None], gtok[None], ggate[None], gwt.reshape(X * WR, D)


def solution(mesh, y_size=4):
    in_specs = (
        P("dp", "context", None),
        P("context", None),
        P("dp", "context", None),
        P(),
        P("context", None, None),
        P("context", None, None),
        P(None, "context", None),
        P("context", None, None),
        P("context", None, None),
        P("dp", "context", None),
    )
    out_specs = (
        P("dp", "context", None),
        P("dp", "context", None),
        P("dp", "context", None),
        P("context", None),
    )
    return jax.shard_map(
        functools.partial(per_device, y_size, mesh.shape["context"]),
        mesh=mesh, in_specs=in_specs, out_specs=out_specs, check_vma=False,
    )
```

time: 158 us -> 135 us (0.85)
  Pallas kernels: 148 us -> 129 us
  local copies, waits for them, and re-layouts: 8.32 us -> 4.62 us
    pallas_call x1, Pallas kernels: 148 us -> 127 us  [per_device(): pl.pallas_call(functools.partial(kernel, Y), out_shape=(jax.ShapeDtypeStr...]
    pallas_call x0 -> x1, Pallas kernels: none -> 2.28 us  [per_device(): pl.pallas_call(finish, grid=(X,), out_shape=(jax.ShapeDtypeStruct((rows,...]
    reshape x1 -> x0, local copies, waits for them, and re-layouts: 2.13 us -> none  [per_device(): kern.reshape(Q * SL, D)]
    unnamed x10 -> x12, local copies, waits for them, and re-layouts: 6.19 us -> 4.62 us
where the time goes in v2:
time: 135 us
  Pallas kernels  129 us (96%)
  local copies, waits for them, and re-layouts  4.62 us (3%)
    pallas_call x1, Pallas kernels, per_device(): pl.pallas_call(functools.partial(kernel, Y), out_shape=(jax.ShapeDtypeStr...  127 us
    unnamed x12, local copies, waits for them, and re-layouts  4.62 us

profile of v2, /device:TPU:1, one launch (start us, length us, event | category | flops | bytes accessed | tf_op | source)
XLA Modules:
  0.0 134.6 jit_solution(14488733732786004427)
XLA Ops:
  0.6 0.0 copy-start
  0.6 0.0 copy-start.1
  0.7 127.0 %shard_map.129 = (bf16[256,2048]{1,0:T(8,128)(2,1)}, bf16[256,2048]{1,0:T(8,128)(2,1)}, bf16[256,2048]{1,0:T(8,128)(2,1)}, bf16[8,16,1024]{2,1,0:T(8,128)(2,1)}) custom-call(bf16[256,2048]{1,0:T(8,128)(2,1)} %bitcast.13, bf16[4,16,2048]{2,1,0:T(8,128)(2,1)} %bitcast.18, bf16[256,2048]{1,0:T(8,128)(2,1)} %bitcast.9, f32[1,2048]{1,0:T(1,128)} %bitcast.19, ...), custom_call_target="tpu_custom_call" | custom-call | flops 8589934592 | bytes 8388608 | tf_op jit(solution)/shard_map/pallas_call | solution.py:485
  127.7 0.0 copy-done
  127.7 0.0 copy-done.1
  127.7 0.0 copy-start.2
  127.7 1.2 copy-done.2
  128.9 0.0 copy-start.3
  128.9 1.2 copy-done.3
  130.2 0.0 copy-start.4
  130.2 1.2 copy-done.4
  131.4 0.0 copy-start.5
  131.4 0.9 copy-done.5
  132.3 2.3 %shard_map.130 = (bf16[256,2048]{1,0:T(8,128)(2,1)}, bf16[256,2048]{1,0:T(8,128)(2,1)}, bf16[256,2048]{1,0:T(8,128)(2,1)}, f32[4,16,2048]{2,1,0:T(8,128)}) custom-call(bf16[256,2048]{1,0:T(8,128)(2,1)S(1)} %copy-done.2, bf16[256,2048]{1,0:T(8,128)(2,1)S(1)} %bitcast.10, bf16[256,2048]{1,0:T(8,128)(2,1)S(1)} %bitcast.12, bf16[256,2048]{1,0:T(8,128)(2,1)S(1)} %copy-done.3, ...), custom_call_target="tpu_custom_call" | custom-call | flops 4194304 | bytes 8388608 | tf_op jit(solution)/shard_map/pallas_call | solution.py:555
Async XLA Ops:
  0.6 127.1 %copy-start = (bf16[1,256,2048]{2,1,0:T(8,128)(2,1)S(1)}, bf16[1,256,2048]{2,1,0:T(8,128)(2,1)}, u32[]{:S(2)}) copy-start(bf16[1,256,2048]{2,1,0:T(8,128)(2,1)} %param.12) | copy-start | bytes 3145732
  0.6 127.1 %copy-start.1 = (bf16[1,256,2048]{2,1,0:T(8,128)(2,1)S(1)}, bf16[1,256,2048]{2,1,0:T(8,128)(2,1)}, u32[]{:S(2)}) copy-start(bf16[1,256,2048]{2,1,0:T(8,128)(2,1)} %param.19) | copy-start | bytes 3145732
  127.7 1.2 copy-start.2
  128.9 1.2 copy-start.3
  130.2 1.2 copy-start.4
  131.4 0.9 copy-start.5

commit v3 on v2

--- a/solution.py
+++ b/solution.py
@@ -163,15 +163,31 @@
         for b in range(2):
             dst[b * Q * SL:(b + 1) * Q * SL, :] = jnp.where(owner == b, full, 0.0).astype(BF)
 
-    def a2a_start(ph, c):
-        def send(d):
-            kk = lax.rem(k + d, CTX)
+    def a2a_send(ph, c, lo, hi, step):
+        def send(i):
+            kk = lax.rem(k + i * step + 1, CTX)
             remote(
                 sb.at[ph, c, kk], rb.at[ph, c, k], s_a2a.at[ph, c], r_a2a.at[ph, c], (dp, kk)
             ).start()
 
-        loop(1, CTX, send)
+        loop(lo, hi, send)
+
+    def a2a_start(ph, c):
+        a2a_send(ph, c, 0, CTX - 1, 1)
         rb[ph, c, k] = sb[ph, c, k]
+
+    def a2a_start_odd(ph, c):
+        a2a_send(ph, c, 0, CTX // 2, 2)
+        rb[ph, c, k] = sb[ph, c, k]
+
+    def a2a_start_even(ph, c):
+        def send(i):
+            kk = lax.rem(k + 2 * i, CTX)
+            remote(
+                sb.at[ph, c, kk], rb.at[ph, c, k], s_a2a.at[ph, c], r_a2a.at[ph, c], (dp, kk)
+            ).start()
+
+        loop(1, CTX // 2, send)
 
     def a2a_desc(ph, c):
         most = pl.ds(0, CTX - 1)
@@ -191,11 +207,6 @@
 
     row_matrix(a4t, f4, True)
 
-    for c in range(NC):
-        c_g[c].wait_recv()
-        put(0, c, mm(a4t[...], g[c].reshape(M, CW)))
-        a2a_start(0, c)
-
     def ag_y(c):
         ag_z_desc(c).wait_recv()
         in_w[c].wait()
@@ -213,6 +224,9 @@
         return remote(wb.at[c, :, ys, x], wb.at[c, :, ys, x], s_ag.at[1, c], r_ag.at[1, c], pdev)
 
     for c in range(NC):
+        c_g[c].wait_recv()
+        put(0, c, mm(a4t[...], g[c].reshape(M, CW)))
+        a2a_start(0, c)
         ag_y(c)
     c_tok = remote(tok, tother, s_pair.at[NC], r_pair.at[NC], pdev)
     c_tok.start()
@@ -255,7 +269,10 @@
         a2a_desc(2, c).wait_recv()
         fl = filtered(mm(a2[...], got(2, c)), c)
         put(3, c, mm_ta(a3t[...], fl))
-        a2a_start(3, c)
+        if c < NC - 1:
+            a2a_start(3, c)
+        else:
+            a2a_start_odd(3, c)
 
     def project(c):
         c_xr2[c].wait_recv()
@@ -411,6 +428,7 @@
         forward_columns(c)
         rs_z(c - 1)
         rs_y(c)
+    a2a_start_even(3, NC - 1)
 
     def gt_own(i):
         gto[:, pl.ds(pl.multiple_of(i * TI, TI), TI)] = token_rows(i, h)
@@ -485,13 +503,13 @@
     pre, gtown, gtr, gfin = pl.pallas_call(
         functools.partial(kernel, Y),
         out_shape=(
-            jax.ShapeDtypeStruct((rows, D), BF),
-            jax.ShapeDtypeStruct((rows, D), BF),
-            jax.ShapeDtypeStruct((rows, D), BF),
-            jax.ShapeDtypeStruct((2 * X, WR, HC), BF),
+            pltpu.VMEM((rows, D), BF),
+            pltpu.VMEM((rows, D), BF),
+            pltpu.VMEM((rows, D), BF),
+            pltpu.VMEM((2 * X, WR, HC), BF),
         ),
         in_specs=[hbm, hbm, hbm, vm, vm, vm, hbm, vm, vm, hbm],
-        out_specs=(hbm,) * 4,
+        out_specs=(vm,) * 4,
         scratch_shapes=[
             pltpu.VMEM((rows, D), BF),
             pltpu.VMEM((rows, D), BF),
@@ -532,7 +550,7 @@
             pltpu.SemaphoreType.DMA((2 * NC + 6,)),
         ],
         compiler_params=pltpu.CompilerParams(
-            collective_id=0, has_side_effects=True, vmem_limit_bytes=60 * 1024 * 1024
+            collective_id=0, has_side_effects=True, vmem_limit_bytes=52 * 1024 * 1024
         ),
         cost_estimate=pl.CostEstimate(
             flops=8 * rows * D * D, bytes_accessed=8 * rows * D * 2, transcendentals=0

time: 135 us -> 128 us (0.948)
  local copies, waits for them, and re-layouts: 4.62 us -> 0.01 us
  Pallas kernels: 129 us -> 127 us
    unnamed x12 -> x4, local copies, waits for them, and re-layouts: 4.62 us -> 0.01 us
    pallas_call x1, Pallas kernels: 127 us -> 125 us  [per_device(): pl.pallas_call(functools.partial(kernel, Y), out_shape=(pltpu.VMEM((rows,...]
where the time goes in v3:
time: 128 us
  Pallas kernels  127 us (99%)
    pallas_call x1, Pallas kernels, per_device(): pl.pallas_call(functools.partial(kernel, Y), out_shape=(pltpu.VMEM((rows,...  125 us

profile of v3, /device:TPU:1, one launch (start us, length us, event | category | flops | bytes accessed | tf_op | source)
XLA Modules:
  0.0 127.9 jit_solution(2938689433951242661)
XLA Ops:
  0.6 0.0 copy-start
  0.6 0.0 copy-start.1
  0.7 124.9 %shard_map.129 = (bf16[256,2048]{1,0:T(8,128)(2,1)S(1)}, bf16[256,2048]{1,0:T(8,128)(2,1)S(1)}, bf16[256,2048]{1,0:T(8,128)(2,1)S(1)}, bf16[8,16,1024]{2,1,0:T(8,128)(2,1)S(1)}) custom-call(bf16[256,2048]{1,0:T(8,128)(2,1)} %bitcast.13, bf16[4,16,2048]{2,1,0:T(8,128)(2,1)} %bitcast.18, bf16[256,2048]{1,0:T(8,128)(2,1)} %bitcast.9, f32[1,2048]{1,0:T(1,128)} %bitcast.19, ...), custom_call_target="tpu_custom_call" | custom-call | flops 8589934592 | bytes 8388608 | tf_op jit(solution)/shard_map/pallas_call | solution.py:503
  125.6 0.0 copy-done
  125.6 0.0 copy-done.1
  125.6 2.3 %shard_map.130 = (bf16[256,2048]{1,0:T(8,128)(2,1)}, bf16[256,2048]{1,0:T(8,128)(2,1)}, bf16[256,2048]{1,0:T(8,128)(2,1)}, f32[4,16,2048]{2,1,0:T(8,128)}) custom-call(bf16[256,2048]{1,0:T(8,128)(2,1)S(1)} %get-tuple-element.12.pre, bf16[256,2048]{1,0:T(8,128)(2,1)S(1)} %bitcast.10, bf16[256,2048]{1,0:T(8,128)(2,1)S(1)} %bitcast.12, ...), custom_call_target="tpu_custom_call" | custom-call | flops 4194304 | bytes 8388608 | tf_op jit(solution)/shard_map/pallas_call | solution.py:573
Async XLA Ops:
  0.6 125.0 %copy-start = (bf16[1,256,2048]{2,1,0:T(8,128)(2,1)S(1)}, bf16[1,256,2048]{2,1,0:T(8,128)(2,1)}, u32[]{:S(2)}) copy-start(bf16[1,256,2048]{2,1,0:T(8,128)(2,1)} %param.12) | copy-start | bytes 3145732
  0.6 125.0 %copy-start.1 = (bf16[1,256,2048]{2,1,0:T(8,128)(2,1)S(1)}, bf16[1,256,2048]{2,1,0:T(8,128)(2,1)}, u32[]{:S(2)}) copy-start(bf16[1,256,2048]{2,1,0:T(8,128)(2,1)} %param.19) | copy-start | bytes 3145732

commit v4 on v3

--- a/solution.py
+++ b/solution.py
@@ -40,9 +40,9 @@
 
 def kernel(
     Y,
-    tok, wgt, gate, skip, f1, f2, kern, f3, f4, cot,
+    tok, wgt, gate, skip_in, f1_in, f2_in, kern, f3_in, f4_in, cot,
     pre, gtown, gtr, gfin,
-    tk, tother, gv, cv, kv, g, gx, gp, p, wb, gw, sb, rb, rxa, rxc, sx, ry, sy, rz, fin,
+    f1, f2, f3, f4, skip, a4, tk, tother, gv, cv, kv, g, gx, gp, p, wb, gw, sb, rb, rxa, rxc, sx, ry, sy, rz, fin,
     a1, a2, a3t, a4t, u, gts, gto, pgo,
     s_ag, r_ag, s_pair, r_pair, s_a2a, r_a2a, s_rs, r_rs, s_loc,
 ):
@@ -89,20 +89,26 @@
     in_kern = local(kern.at[:, :, pl.ds(half, HC)], kv, 2)
     in_tok = local(tok, tk, 3)
     in_w = [local(wgt.at[x, :, mine(c)], wb.at[c, z, y, x], 4 + c) for c in range(NC)]
+    small = [
+        local(src, dst, 6 + 2 * NC + i)
+        for i, (src, dst) in enumerate(
+            ((f4_in, f4), (f3_in, f3), (f2_in, f2), (f1_in, f1), (skip_in, skip))
+        )
+    ]
+
+    barrier = pltpu.get_barrier_semaphore()
+
+    def greet_context(d):
+        pl.semaphore_signal(barrier, inc=1, device_id=(dp, lax.rem(k + d, CTX)), device_id_type=MESH)
+
+    def greet_dp(d):
+        pl.semaphore_signal(barrier, inc=1, device_id=(lax.rem(dp + d, DP), k), device_id_type=MESH)
+
+    loop(1, CTX, greet_context)
+    loop(1, DP, greet_dp)
     in_gate.start()
     in_cot.start()
-
-    barrier = pltpu.get_barrier_semaphore()
-
-    def greet_context(d):
-        pl.semaphore_signal(barrier, inc=1, device_id=(dp, lax.rem(k + d, CTX)), device_id_type=MESH)
-
-    def greet_dp(d):
-        pl.semaphore_signal(barrier, inc=1, device_id=(lax.rem(dp + d, DP), k), device_id_type=MESH)
-
-    loop(1, DP, greet_dp)
-    loop(1, CTX, greet_context)
-    for copy in in_w:
+    for copy in small + in_w:
         copy.start()
     in_kern.start()
     in_tok.start()
@@ -205,23 +211,32 @@
     def cols(c):
         return slice(c * CW, (c + 1) * CW)
 
+    small[0].wait()
     row_matrix(a4t, f4, True)
+
+    near = sorted(range(1, Y), key=lambda d: min(d, Y - d))
+
+    def ag_y_copy(c, d):
+        to = (dp, z * Y + lax.rem(y + d, Y))
+        return remote(wb.at[c, :, y, x], wb.at[c, :, y, x], s_ag.at[d, c], r_ag.at[d, c], to)
+
+    def ag_x1_copies(c, d):
+        block = wb.at[c, :, lax.rem(y - d + Y, Y), x]
+        return (
+            remote(block, block, s_ag.at[Y + d, c], r_ag.at[Y + d, c], rdev),
+            remote(block, block, s_ag.at[2 * Y + d, c], r_ag.at[2 * Y + d, c], ldev),
+        )
+
+    def ag_x1_send(c, d):
+        for copy in ag_x1_copies(c, d):
+            copy.start()
 
     def ag_y(c):
         ag_z_desc(c).wait_recv()
         in_w[c].wait()
-
-        def send(d):
-            yy = lax.rem(y + d, Y)
-            remote(
-                wb.at[c, :, y, x], wb.at[c, :, y, x], s_ag.at[1, c], r_ag.at[1, c], (dp, z * Y + yy)
-            ).start()
-
-        loop(1, Y, send)
-
-    def ag_y_desc(c):
-        ys = pl.ds(0, Y - 1)
-        return remote(wb.at[c, :, ys, x], wb.at[c, :, ys, x], s_ag.at[1, c], r_ag.at[1, c], pdev)
+        for d in near:
+            ag_y_copy(c, d).start()
+        ag_x1_send(c, 0)
 
     for c in range(NC):
         c_g[c].wait_recv()
@@ -230,23 +245,32 @@
         ag_y(c)
     c_tok = remote(tok, tother, s_pair.at[NC], r_pair.at[NC], pdev)
     c_tok.start()
+    for copy in small[1:]:
+        copy.wait()
     column_matrix(a3t, f3, True)
 
     lo, hi = pl.ds(0, ZH), pl.ds(ZH, Z - ZH)
-    c_xr = [remote(wb.at[c, :, :, x], wb.at[c, :, :, x], s_ag.at[2, c], r_ag.at[2, c], rdev) for c in range(NC)]
-    c_xl = [remote(wb.at[c, :, :, x], wb.at[c, :, :, x], s_ag.at[3, c], r_ag.at[3, c], ldev) for c in range(NC)]
-    c_xr2 = [remote(wb.at[c, lo, :, left], wb.at[c, lo, :, left], s_ag.at[4, c], r_ag.at[4, c], rdev) for c in range(NC)]
-    c_xl2 = [remote(wb.at[c, hi, :, right], wb.at[c, hi, :, right], s_ag.at[5, c], r_ag.at[5, c], ldev) for c in range(NC)]
+    last = 3 * Y
+    c_xr2 = [
+        remote(wb.at[c, lo, :, left], wb.at[c, lo, :, left], s_ag.at[last, c], r_ag.at[last, c], rdev)
+        for c in range(NC)
+    ]
+    c_xl2 = [
+        remote(wb.at[c, hi, :, right], wb.at[c, hi, :, right], s_ag.at[last + 1, c], r_ag.at[last + 1, c], ldev)
+        for c in range(NC)
+    ]
 
     def ag_x1(c):
-        ag_y_desc(c).wait_recv()
-        c_xr[c].start()
-        c_xl[c].start()
+        for d in near:
+            ag_y_copy(c, d).wait_recv()
+            ag_x1_send(c, d)
 
     def ag_x2(c):
-        c_xr[c].wait_recv()
+        for d in range(Y):
+            ag_x1_copies(c, d)[0].wait_recv()
         c_xr2[c].start()
-        c_xl[c].wait_recv()
+        for d in range(Y):
+            ag_x1_copies(c, d)[1].wait_recv()
         c_xl2[c].start()
 
     ag_x1(0)
@@ -254,6 +278,7 @@
     for c in range(1, NC):
         ag_x1(c)
     row_matrix(a1, f1, False)
+    a4[...] = a4t[...].T
 
     def filtered(value, c):
         kc = kv[:, :, cols(c)].astype(F32).reshape(Q * SL, CW)
@@ -263,16 +288,11 @@
         a2a_desc(0, c).wait_recv()
         gs = filtered(mm(a3t[...], got(0, c)), c)
         put(1, c, mm_ta(a2[...], gs))
-        a2a_start(1, c)
 
     def forward_columns(c):
         a2a_desc(2, c).wait_recv()
         fl = filtered(mm(a2[...], got(2, c)), c)
         put(3, c, mm_ta(a3t[...], fl))
-        if c < NC - 1:
-            a2a_start(3, c)
-        else:
-            a2a_start_odd(3, c)
 
     def project(c):
         c_xr2[c].wait_recv()
@@ -286,36 +306,49 @@
         gf = mm_ta(a1[...], got(1, c)) + skip[:, mine(c)] * g[c].reshape(M, CW).astype(F32)
         gp[c] = gf.astype(BF).reshape(2, rows, CW)
 
-    def rs_copies(c):
-        return (
-            remote(gw.at[c, lo, :, opp], rxa.at[c, 0], s_rs.at[0, c], r_rs.at[0, c], rdev),
-            remote(gw.at[c, hi, :, opp], rxa.at[c, 1], s_rs.at[1, c], r_rs.at[1, c], ldev),
-            remote(gw.at[c, hi, :, right], rxc.at[c, 0, hi], s_rs.at[2, c], r_rs.at[2, c], rdev),
-            remote(gw.at[c, lo, :, left], rxc.at[c, 1, lo], s_rs.at[3, c], r_rs.at[3, c], ldev),
-            remote(gw.at[c, lo, :, right], rxc.at[c, 0, lo], s_rs.at[4, c], r_rs.at[4, c], rdev),
-            remote(gw.at[c, hi, :, left], rxc.at[c, 1, hi], s_rs.at[5, c], r_rs.at[5, c], ldev),
+    def rs_copies(c, own):
+        yb = pl.ds(0, 1) if own else pl.ds(1, Y - 1)
+        at = 6 if own else 0
+        moves = (
+            (gw.at[c, lo, yb, opp], rxa.at[c, 0, :, yb], rdev),
+            (gw.at[c, hi, yb, opp], rxa.at[c, 1, :, yb], ldev),
+            (gw.at[c, hi, yb, right], rxc.at[c, 0, hi, yb], rdev),
+            (gw.at[c, lo, yb, left], rxc.at[c, 1, lo, yb], ldev),
+            (gw.at[c, lo, yb, right], rxc.at[c, 0, lo, yb], rdev),
+            (gw.at[c, hi, yb, left], rxc.at[c, 1, hi, yb], ldev),
         )
+        return [
+            remote(src, dst, s_rs.at[at + i, c], r_rs.at[at + i, c], dev)
+            for i, (src, dst, dev) in enumerate(moves)
+        ]
 
     def rs_x1(c):
         def part_rows(i):
             at = pl.ds(pl.multiple_of(i * TI, TI), TI)
             part = mm_ta(tk[:, at], gp[c, h]) + mm_ta(tother[:, at], gp[c, other])
-            gw[c, i] = part.astype(BF).reshape(Y, X, WR, CW)
+            part = part.astype(BF).reshape(Y, X, WR, CW)
+            for yy in range(Y):
+                gw[c, i, lax.rem(yy - y + Y, Y)] = part[yy]
 
         loop(0, Z, part_rows)
-        for copy in rs_copies(c)[:4]:
+        for copy in rs_copies(c, False)[:4]:
             copy.start()
 
-    def rs_x2(c):
-        copies = rs_copies(c)
+    def rs_pass(c, own):
+        copies = rs_copies(c, own)
+        blocks = range(0, 1) if own else range(1, Y)
 
         def add_right(i):
-            gw[c, i, :, right] = (gw[c, i, :, right].astype(F32) + rxa[c, 0, i].astype(F32)).astype(BF)
+            for r in blocks:
+                gw[c, i, r, right] = (
+                    gw[c, i, r, right].astype(F32) + rxa[c, 0, i, r].astype(F32)
+                ).astype(BF)
 
         def add_left(i):
-            gw[c, ZH + i, :, left] = (
-                gw[c, ZH + i, :, left].astype(F32) + rxa[c, 1, i].astype(F32)
-            ).astype(BF)
+            for r in blocks:
+                gw[c, ZH + i, r, left] = (
+                    gw[c, ZH + i, r, left].astype(F32) + rxa[c, 1, i, r].astype(F32)
+                ).astype(BF)
 
         copies[0].wait_recv()
         loop(0, ZH, add_right)
@@ -324,33 +357,43 @@
         loop(0, ZH, add_left)
         copies[5].start()
 
+    def rs_x2(c):
+        rs_pass(c, False)
+        for copy in rs_copies(c, True)[:4]:
+            copy.start()
+
+    def rs_x3(c):
+        rs_pass(c, True)
+
+    def sum_x(c, own):
+        for copy in rs_copies(c, own)[2:]:
+            copy.wait_recv()
+        blocks = range(0, 1) if own else range(1, Y)
+
+        def add(i):
+            for r in blocks:
+                sx[c, i, r] = (
+                    gw[c, i, r, x].astype(F32) + rxc[c, 0, i, r].astype(F32) + rxc[c, 1, i, r].astype(F32)
+                ).astype(BF)
+
+        loop(0, Z, add)
+
+    def rs_y_copy(c, d):
+        to = (dp, z * Y + lax.rem(y + d, Y))
+        return remote(sx.at[c, :, d], ry.at[c, d - 1], s_rs.at[11 + d, c], r_rs.at[11 + d, c], to)
+
     def rs_y(c):
-        for copy in rs_copies(c)[2:]:
-            copy.wait_recv()
-
-        def sum_x(i):
-            sx[c, i] = (
-                gw[c, i, :, x].astype(F32) + rxc[c, 0, i].astype(F32) + rxc[c, 1, i].astype(F32)
-            ).astype(BF)
-
-        loop(0, Z, sum_x)
-
-        def send(d):
-            yy = lax.rem(y + d, Y)
-            remote(
-                sx.at[c, :, yy], ry.at[c, d - 1], s_rs.at[6, c], r_rs.at[6, c], (dp, z * Y + yy)
-            ).start()
-
-        loop(1, Y, send)
-
-    def rs_y_desc(c):
-        return remote(ry.at[c], ry.at[c], s_rs.at[6, c], r_rs.at[6, c], pdev)
+        sum_x(c, False)
+        for d in near:
+            rs_y_copy(c, d).start()
 
     def rs_z(c):
-        rs_y_desc(c).wait_recv()
+        sum_x(c, True)
+        for d in near:
+            rs_y_copy(c, d).wait_recv()
 
         def sum_y(i):
-            total = sx[c, i, y].astype(F32)
+            total = sx[c, i, 0].astype(F32)
             for d in range(Y - 1):
                 total = total + ry[c, d, i].astype(F32)
             sy[c, i] = total.astype(BF)
@@ -360,13 +403,13 @@
         def send(d):
             zz = lax.rem(z + d, Z)
             remote(
-                sy.at[c, zz], rz.at[c, d - 1], s_rs.at[7, c], r_rs.at[7, c], (dp, zz * Y + y)
+                sy.at[c, zz], rz.at[c, d - 1], s_rs.at[11 + Y, c], r_rs.at[11 + Y, c], (dp, zz * Y + y)
             ).start()
 
         loop(1, Z, send)
 
     def rs_z_desc(c):
-        return remote(rz.at[c], rz.at[c], s_rs.at[7, c], r_rs.at[7, c], pdev)
+        return remote(rz.at[c], rz.at[c], s_rs.at[11 + Y, c], r_rs.at[11 + Y, c], pdev)
 
     def rs_sum(c):
         rs_z_desc(c).wait_recv()
@@ -377,7 +420,7 @@
 
     def field_rows(c):
         a2a_desc(3, c).wait_recv()
-        front = mm_ta(a4t[...], got(3, c)) + skip[:, mine(c)] * p[c].reshape(M, CW).astype(F32)
+        front = mm(a4[...], got(3, c)) + skip[:, mine(c)] * p[c].reshape(M, CW).astype(F32)
         pgo[c] = front.astype(BF).reshape(2, rows, CW)
 
     out_pre = [local(pgo.at[c, h], pre.at[:, mine(c)], 4 + NC + c) for c in range(NC)]
@@ -387,26 +430,25 @@
     ]
 
     in_kern.wait()
-    back_columns(0)
-    ag_x2(0)
-    for c in range(1, NC):
+    for c in range(NC):
         back_columns(c)
         ag_x2(c)
+        a2a_start(1, c)
     in_tok.wait()
     c_tok.wait_recv()
     project(0)
 
     a2a_desc(1, 0).wait_recv()
-    a2a_start(2, 0)
     gradient_rows(0)
     rs_x1(0)
+    a2a_start(2, 0)
     for c in range(1, NC):
         project(c)
         rs_x2(c - 1)
         a2a_desc(1, c).wait_recv()
-        a2a_start(2, c)
         gradient_rows(c)
         rs_x1(c)
+        a2a_start(2, c)
 
     def token_rows(i, b):
         total = mm_tb(gp[0, b], wb[0, i].reshape(TI, CW))
@@ -421,12 +463,17 @@
     c_gt = remote(gts, gtr, s_pair.at[NC + 1], r_pair.at[NC + 1], pdev)
     c_gt.start()
 
+    rs_x3(0)
     forward_columns(0)
     rs_x2(NC - 1)
+    a2a_start_odd(3, 0)
     rs_y(0)
+    a2a_start_even(3, 0)
+    rs_x3(NC - 1)
     for c in range(1, NC):
         forward_columns(c)
         rs_z(c - 1)
+        a2a_start_odd(3, c)
         rs_y(c)
     a2a_start_even(3, NC - 1)
 
@@ -447,7 +494,7 @@
     my_rows = gfin.at[dp]
 
     def share(d):
-        remote(fin, my_rows, s_rs.at[8, 0], r_rs.at[8, 0], (lax.rem(dp + d, DP), k)).start()
+        remote(fin, my_rows, s_rs.at[12 + Y, 0], r_rs.at[12 + Y, 0], (lax.rem(dp + d, DP), k)).start()
 
     loop(1, DP, share)
     out_fin = local(fin, my_rows, 5 + 2 * NC)
@@ -456,18 +503,24 @@
     out_pre[NC - 1].start()
     c_pre[NC - 1].start()
     share_desc = remote(
-        gfin.at[pl.ds(0, DP - 1)], gfin.at[pl.ds(0, DP - 1)], s_rs.at[8, 0], r_rs.at[8, 0], pdev
+        gfin.at[pl.ds(0, DP - 1)], gfin.at[pl.ds(0, DP - 1)], s_rs.at[12 + Y, 0], r_rs.at[12 + Y, 0], pdev
     )
 
     for c in range(NC):
         out_pre[c].wait()
         c_pre[c].wait()
         c_g[c].wait_send()
-        for copy in (c_xr[c], c_xl[c], c_xr2[c], c_xl2[c], ag_z_desc(c), ag_y_desc(c)):
+        for copy in (c_xr2[c], c_xl2[c], ag_z_desc(c)):
             copy.wait_send()
-        for copy in rs_copies(c):
+        for d in range(Y):
+            for copy in ag_x1_copies(c, d):
+                copy.wait_send()
+        for d in near:
+            ag_y_copy(c, d).wait_send()
+        for copy in rs_copies(c, False) + rs_copies(c, True):
             copy.wait_send()
-        rs_y_desc(c).wait_send()
+        for d in near:
+            rs_y_copy(c, d).wait_send()
         rs_z_desc(c).wait_send()
         for ph in range(4):
             a2a_desc(ph, c).wait_send()
@@ -508,9 +561,15 @@
             pltpu.VMEM((rows, D), BF),
             pltpu.VMEM((2 * X, WR, HC), BF),
         ),
-        in_specs=[hbm, hbm, hbm, vm, vm, vm, hbm, vm, vm, hbm],
+        in_specs=[hbm] * 10,
         out_specs=(vm,) * 4,
         scratch_shapes=[
+            pltpu.VMEM((first.shape[0], R, R), BF),
+            pltpu.VMEM((SL, Q, Q), BF),
+            pltpu.VMEM((SL, Q, Q), BF),
+            pltpu.VMEM((first.shape[0], R, R), BF),
+            pltpu.VMEM((1, D), F32),
+            pltpu.VMEM((M, M), BF),
             pltpu.VMEM((rows, D), BF),
             pltpu.VMEM((rows, D), BF),
             pltpu.VMEM((rows, D), BF),
@@ -539,15 +598,15 @@
             pltpu.VMEM((rows, D), BF),
             pltpu.VMEM((rows, D), BF),
             pltpu.VMEM((NC, 2, rows, CW), BF),
-            pltpu.SemaphoreType.DMA((6, NC)),
-            pltpu.SemaphoreType.DMA((6, NC)),
+            pltpu.SemaphoreType.DMA((3 * Y + 2, NC)),
+            pltpu.SemaphoreType.DMA((3 * Y + 2, NC)),
             pltpu.SemaphoreType.DMA((2 * NC + 2,)),
             pltpu.SemaphoreType.DMA((2 * NC + 2,)),
             pltpu.SemaphoreType.DMA((4, NC)),
             pltpu.SemaphoreType.DMA((4, NC)),
-            pltpu.SemaphoreType.DMA((9, NC)),
-            pltpu.SemaphoreType.DMA((9, NC)),
-            pltpu.SemaphoreType.DMA((2 * NC + 6,)),
+            pltpu.SemaphoreType.DMA((13 + Y, NC)),
+            pltpu.SemaphoreType.DMA((13 + Y, NC)),
+            pltpu.SemaphoreType.DMA((2 * NC + 11,)),
         ],
         compiler_params=pltpu.CompilerParams(
             collective_id=0, has_side_effects=True, vmem_limit_bytes=52 * 1024 * 1024

time: 128 us -> 125 us (0.977)
  Pallas kernels: 127 us -> 124 us
    pallas_call x1, Pallas kernels: 125 us -> 122 us  [per_device(): pl.pallas_call(functools.partial(kernel, Y), out_shape=(pltpu.VMEM((rows,...]
where the time goes in v4:
time: 125 us
  Pallas kernels  124 us (99%)
    pallas_call x1, Pallas kernels, per_device(): pl.pallas_call(functools.partial(kernel, Y), out_shape=(pltpu.VMEM((rows,...  122 us

profile of v4, /device:TPU:1, one launch (start us, length us, event | category | flops | bytes accessed | tf_op | source)
XLA Modules:
  0.0 124.9 jit_solution(12544017314649441231)
XLA Ops:
  0.6 0.0 copy-start
  0.6 0.0 copy-start.1
  0.7 121.9 %shard_map.129 = (bf16[256,2048]{1,0:T(8,128)(2,1)S(1)}, bf16[256,2048]{1,0:T(8,128)(2,1)S(1)}, bf16[256,2048]{1,0:T(8,128)(2,1)S(1)}, bf16[8,16,1024]{2,1,0:T(8,128)(2,1)S(1)}) custom-call(bf16[256,2048]{1,0:T(8,128)(2,1)} %bitcast.13, bf16[4,16,2048]{2,1,0:T(8,128)(2,1)} %bitcast.18, bf16[256,2048]{1,0:T(8,128)(2,1)} %bitcast.9, f32[1,2048]{1,0:T(1,128)} %bitcast.19, ...), custom_call_target="tpu_custom_call" | custom-call | flops 8589934592 | bytes 8388608 | tf_op jit(solution)/shard_map/pallas_call | solution.py:556
  122.6 0.0 copy-done
  122.6 0.0 copy-done.1
  122.6 2.3 %shard_map.130 = (bf16[256,2048]{1,0:T(8,128)(2,1)}, bf16[256,2048]{1,0:T(8,128)(2,1)}, bf16[256,2048]{1,0:T(8,128)(2,1)}, f32[4,16,2048]{2,1,0:T(8,128)}) custom-call(bf16[256,2048]{1,0:T(8,128)(2,1)S(1)} %get-tuple-element.12.pre, bf16[256,2048]{1,0:T(8,128)(2,1)S(1)} %bitcast.10, bf16[256,2048]{1,0:T(8,128)(2,1)S(1)} %bitcast.12, ...), custom_call_target="tpu_custom_call" | custom-call | flops 4194304 | bytes 8388608 | tf_op jit(solution)/shard_map/pallas_call | solution.py:632
Async XLA Ops:
  0.6 122.0 %copy-start = (bf16[1,256,2048]{2,1,0:T(8,128)(2,1)S(1)}, bf16[1,256,2048]{2,1,0:T(8,128)(2,1)}, u32[]{:S(2)}) copy-start(bf16[1,256,2048]{2,1,0:T(8,128)(2,1)} %param.12) | copy-start | bytes 3145732
  0.6 122.0 %copy-start.1 = (bf16[1,256,2048]{2,1,0:T(8,128)(2,1)S(1)}, bf16[1,256,2048]{2,1,0:T(8,128)(2,1)}, u32[]{:S(2)}) copy-start(bf16[1,256,2048]{2,1,0:T(8,128)(2,1)} %param.19) | copy-start | bytes 3145732

commit v5 on v4

--- a/solution.py
+++ b/solution.py
@@ -432,8 +432,9 @@
     in_kern.wait()
     for c in range(NC):
         back_columns(c)
+        a2a_start_odd(1, c)
         ag_x2(c)
-        a2a_start(1, c)
+        a2a_start_even(1, c)
     in_tok.wait()
     c_tok.wait_recv()
     project(0)
@@ -470,6 +471,14 @@
     rs_y(0)
     a2a_start_even(3, 0)
     rs_x3(NC - 1)
+
+    def gt_own(i):
+        gto[:, pl.ds(pl.multiple_of(i * TI, TI), TI)] = token_rows(i, h)
+
+    loop(0, Z, gt_own)
+    out_gt = local(gto, gtown, 4 + 2 * NC)
+    out_gt.start()
+
     for c in range(1, NC):
         forward_columns(c)
         rs_z(c - 1)
@@ -477,19 +486,15 @@
         rs_y(c)
     a2a_start_even(3, NC - 1)
 
-    def gt_own(i):
-        gto[:, pl.ds(pl.multiple_of(i * TI, TI), TI)] = token_rows(i, h)
-
-    loop(0, Z, gt_own)
-    out_gt = local(gto, gtown, 4 + 2 * NC)
-    out_gt.start()
-
     for c in range(NC - 1):
         rs_sum(c)
         field_rows(c)
         out_pre[c].start()
         c_pre[c].start()
     rs_z(NC - 1)
+    field_rows(NC - 1)
+    out_pre[NC - 1].start()
+    c_pre[NC - 1].start()
     rs_sum(NC - 1)
     my_rows = gfin.at[dp]
 
@@ -499,9 +504,6 @@
     loop(1, DP, share)
     out_fin = local(fin, my_rows, 5 + 2 * NC)
     out_fin.start()
-    field_rows(NC - 1)
-    out_pre[NC - 1].start()
-    c_pre[NC - 1].start()
     share_desc = remote(
         gfin.at[pl.ds(0, DP - 1)], gfin.at[pl.ds(0, DP - 1)], s_rs.at[12 + Y, 0], r_rs.at[12 + Y, 0], pdev
     )
@@ -531,14 +533,30 @@
     share_desc.wait()
 
 
-def finish(pre, gate, cot, gtown, gtr, gfin, mixed, gtok, ggate, gwt):
-    front = pre[...].astype(F32)
-    mixed[...] = (gate[...].astype(F32) * front).astype(BF)
-    ggate[...] = (cot[...].astype(F32) * front).astype(BF)
-    gtok[...] = (gtown[...].astype(F32) + gtr[...].astype(F32)).astype(BF)
+def finish(pre, gate, cot, gtown, gtr, gfin, mixed, gtok, ggate, gwt, mv, tv, gv, wv, sems):
+    rows, D = pre.shape
     HC = gfin.shape[2]
-    for j in range(2):
-        gwt[0, :, j * HC:(j + 1) * HC] = gfin[j].astype(F32)
+    part = rows // X
+    copies = []
+    for i in range(X):
+        r = slice(i * part, (i + 1) * part)
+        at = pl.ds(i * part, part)
+        front = pre[r].astype(F32)
+        mv[r] = (gate[r].astype(F32) * front).astype(BF)
+        copies.append(pltpu.make_async_copy(mv.at[at], mixed.at[at], sems.at[4 * i]))
+        copies[-1].start()
+        gv[r] = (cot[r].astype(F32) * front).astype(BF)
+        copies.append(pltpu.make_async_copy(gv.at[at], ggate.at[at], sems.at[4 * i + 1]))
+        copies[-1].start()
+        tv[r] = (gtown[r].astype(F32) + gtr[r].astype(F32)).astype(BF)
+        copies.append(pltpu.make_async_copy(tv.at[at], gtok.at[at], sems.at[4 * i + 2]))
+        copies[-1].start()
+        for j in range(2):
+            wv[i, :, j * HC:(j + 1) * HC] = gfin[2 * i + j].astype(F32)
+        copies.append(pltpu.make_async_copy(wv.at[i], gwt.at[i], sems.at[4 * i + 3]))
+        copies[-1].start()
+    for copy in copies:
+        copy.wait()
 
 
 def per_device(Y, CTX, tokens, weight, gate, skip, first, second, kern, third, fourth, cotangent):
@@ -626,20 +644,23 @@
         fourth,
         cotangent[0],
     )
-    block = pl.BlockSpec((rows // X, D), lambda i: (i, 0))
-    wide = pl.BlockSpec((1, WR, D), lambda i: (i, 0, 0))
-    two = pl.BlockSpec((2, WR, HC), lambda i: (i, 0, 0))
     mixed, gtok, ggate, gwt = pl.pallas_call(
         finish,
-        grid=(X,),
         out_shape=(
             jax.ShapeDtypeStruct((rows, D), BF),
             jax.ShapeDtypeStruct((rows, D), BF),
             jax.ShapeDtypeStruct((rows, D), BF),
             jax.ShapeDtypeStruct((X, WR, D), F32),
         ),
-        in_specs=[block, block, block, block, block, two],
-        out_specs=(block, block, block, wide),
+        in_specs=[vm] * 6,
+        out_specs=(hbm,) * 4,
+        scratch_shapes=[
+            pltpu.VMEM((rows, D), BF),
+            pltpu.VMEM((rows, D), BF),
+            pltpu.VMEM((rows, D), BF),
+            pltpu.VMEM((X, WR, D), F32),
+            pltpu.SemaphoreType.DMA((4 * X,)),
+        ],
         compiler_params=pltpu.CompilerParams(vmem_limit_bytes=16 * 1024 * 1024),
         cost_estimate=pl.CostEstimate(
             flops=8 * rows * D, bytes_accessed=16 * rows * D, transcendentals=0

time: 125 us -> 124 us (level)
  no operation moved by 1% of the time
where the time goes in v5:
time: 124 us
  Pallas kernels  123 us (99%)
    pallas_call x1, Pallas kernels, per_device(): pl.pallas_call(functools.partial(kernel, Y), out_shape=(pltpu.VMEM((rows,...  121 us

profile of v5, /device:TPU:1, one launch (start us, length us, event | category | flops | bytes accessed | tf_op | source)
XLA Modules:
  0.0 124.1 jit_solution(6761703034699380440)
XLA Ops:
  0.6 0.0 copy-start
  0.6 0.0 copy-start.1
  0.7 121.4 %shard_map.129 = (bf16[256,2048]{1,0:T(8,128)(2,1)S(1)}, bf16[256,2048]{1,0:T(8,128)(2,1)S(1)}, bf16[256,2048]{1,0:T(8,128)(2,1)S(1)}, bf16[8,16,1024]{2,1,0:T(8,128)(2,1)S(1)}) custom-call(bf16[256,2048]{1,0:T(8,128)(2,1)} %bitcast.13, bf16[4,16,2048]{2,1,0:T(8,128)(2,1)} %bitcast.18, bf16[256,2048]{1,0:T(8,128)(2,1)} %bitcast.9, f32[1,2048]{1,0:T(1,128)} %bitcast.19, ...), custom_call_target="tpu_custom_call" | custom-call | flops 8589934592 | bytes 8388608 | tf_op jit(solution)/shard_map/pallas_call | solution.py:574
  122.1 0.0 copy-done
  122.1 0.0 copy-done.1
  122.1 2.0 %shard_map.130 = (bf16[256,2048]{1,0:T(8,128)(2,1)}, bf16[256,2048]{1,0:T(8,128)(2,1)}, bf16[256,2048]{1,0:T(8,128)(2,1)}, f32[4,16,2048]{2,1,0:T(8,128)}) custom-call(bf16[256,2048]{1,0:T(8,128)(2,1)S(1)} %get-tuple-element.12.pre, bf16[256,2048]{1,0:T(8,128)(2,1)S(1)} %bitcast.10, bf16[256,2048]{1,0:T(8,128)(2,1)S(1)} %bitcast.12, ...), custom_call_target="tpu_custom_call" | custom-call | flops 4194304 | bytes 8388608 | tf_op jit(solution)/shard_map/pallas_call | solution.py:647
Async XLA Ops:
  0.6 121.4 %copy-start = (bf16[1,256,2048]{2,1,0:T(8,128)(2,1)S(1)}, bf16[1,256,2048]{2,1,0:T(8,128)(2,1)}, u32[]{:S(2)}) copy-start(bf16[1,256,2048]{2,1,0:T(8,128)(2,1)} %param.12) | copy-start | bytes 3145732
  0.6 121.4 %copy-start.1 = (bf16[1,256,2048]{2,1,0:T(8,128)(2,1)S(1)}, bf16[1,256,2048]{2,1,0:T(8,128)(2,1)}, u32[]{:S(2)}) copy-start(bf16[1,256,2048]{2,1,0:T(8,128)(2,1)} %param.19) | copy-start | bytes 3145732

commit v6 on v5

--- a/solution.py
+++ b/solution.py
@@ -440,16 +440,18 @@
     project(0)
 
     a2a_desc(1, 0).wait_recv()
+    a2a_start_odd(2, 0)
     gradient_rows(0)
     rs_x1(0)
-    a2a_start(2, 0)
+    a2a_start_even(2, 0)
     for c in range(1, NC):
         project(c)
         rs_x2(c - 1)
         a2a_desc(1, c).wait_recv()
+        a2a_start_odd(2, c)
         gradient_rows(c)
         rs_x1(c)
-        a2a_start(2, c)
+        a2a_start_even(2, c)
 
     def token_rows(i, b):
         total = mm_tb(gp[0, b], wb[0, i].reshape(TI, CW))

time: 124 us -> 124 us (level)
  no operation moved by 1% of the time
where the time goes in v6:
time: 124 us
  Pallas kernels  124 us (100%)
    pallas_call x1, Pallas kernels, per_device(): pl.pallas_call(functools.partial(kernel, Y), out_shape=(pltpu.VMEM((rows,...  121 us

profile of v6, /device:TPU:1, one launch (start us, length us, event | category | flops | bytes accessed | tf_op | source)
XLA Modules:
  0.0 124.2 jit_solution(17459269557174674353)
XLA Ops:
  0.6 0.0 copy-start
  0.6 0.0 copy-start.1
  0.7 121.5 %shard_map.129 = (bf16[256,2048]{1,0:T(8,128)(2,1)S(1)}, bf16[256,2048]{1,0:T(8,128)(2,1)S(1)}, bf16[256,2048]{1,0:T(8,128)(2,1)S(1)}, bf16[8,16,1024]{2,1,0:T(8,128)(2,1)S(1)}) custom-call(bf16[256,2048]{1,0:T(8,128)(2,1)} %bitcast.13, bf16[4,16,2048]{2,1,0:T(8,128)(2,1)} %bitcast.18, bf16[256,2048]{1,0:T(8,128)(2,1)} %bitcast.9, f32[1,2048]{1,0:T(1,128)} %bitcast.19, ...), custom_call_target="tpu_custom_call" | custom-call | flops 8589934592 | bytes 8388608 | tf_op jit(solution)/shard_map/pallas_call | solution.py:576
  122.2 0.0 copy-done
  122.2 0.0 copy-done.1
  122.2 2.0 %shard_map.130 = (bf16[256,2048]{1,0:T(8,128)(2,1)}, bf16[256,2048]{1,0:T(8,128)(2,1)}, bf16[256,2048]{1,0:T(8,128)(2,1)}, f32[4,16,2048]{2,1,0:T(8,128)}) custom-call(bf16[256,2048]{1,0:T(8,128)(2,1)S(1)} %get-tuple-element.12.pre, bf16[256,2048]{1,0:T(8,128)(2,1)S(1)} %bitcast.10, bf16[256,2048]{1,0:T(8,128)(2,1)S(1)} %bitcast.12, ...), custom_call_target="tpu_custom_call" | custom-call | flops 4194304 | bytes 8388608 | tf_op jit(solution)/shard_map/pallas_call | solution.py:649
Async XLA Ops:
  0.6 121.5 %copy-start = (bf16[1,256,2048]{2,1,0:T(8,128)(2,1)S(1)}, bf16[1,256,2048]{2,1,0:T(8,128)(2,1)}, u32[]{:S(2)}) copy-start(bf16[1,256,2048]{2,1,0:T(8,128)(2,1)} %param.12) | copy-start | bytes 3145732
  0.6 121.5 %copy-start.1 = (bf16[1,256,2048]{2,1,0:T(8,128)(2,1)S(1)}, bf16[1,256,2048]{2,1,0:T(8,128)(2,1)}, u32[]{:S(2)}) copy-start(bf16[1,256,2048]{2,1,0:T(8,128)(2,1)} %param.19) | copy-start | bytes 3145732
